TPU v7x, 128 devices: a whole 4x4x4 slice. The times are simulated.
128 devices in a mesh: grp: 8 (over y, core), dev: 16 (over x, z).
Axes of the slice: x: 4, y: 4, z: 4, core: 2. Of those that a mesh axis runs over, the one named last changes fastest.
Arguments:
- modes: bfloat16 [32, 2097152], P(None, ('grp', 'dev')), may hold values from -6 to 6
- geometry: float32 [4, 2097152], P(None, ('grp', 'dev')), may hold values from -2.4 to 2.4, as said below
- pair_list: int32 [16384, 2], P(('grp', 'dev')), may hold values from 0 to 8191, as said below
- pair_kind: int32 [16384], P(('grp', 'dev')), may hold values from 0 to 2, as said below
Outputs:
- added: float32 [32, 2097152], P(None, ('grp', 'dev'))
Inputs may be any that keep to these rules, and one draw needn't show every extreme that they name: `pair_list`: cluster ids. Of the 256 cluster ids in the slots of one device (empty slots included), at most 2 lie on any one device (cluster c lies on device c // 64 of grp+dev), and every device that holds one of them holds exactly 2. `pair_kind`: on each device the live slots come first; some device has all 128 slots live. `geometry`: rows 0 to 2 lie in -2.4 to 2.4; row 3 lies in 0.1 to 2.
All inputs are finite; a program needn't handle non-finite values.
Results may differ from a plain program's by a relative error of at most 0.0029.
Values may be sent and summed in bfloat16 or wider, within the bound.
A program may use at most 64 MiB of HBM per device.

v0:
```python
import math

import jax
import jax.numpy as jnp
from jax import lax
from jax.sharding import PartitionSpec as P

P_SIZE = 256


KERNEL_SCALE = 0.25 / math.pi


def build_kernel(left_geo, right_geo, factor):
    distance = (left_geo[:, 0, :, None] - right_geo[:, 0, None, :]) ** 2
    distance = distance + (left_geo[:, 1, :, None] - right_geo[:, 1, None, :]) ** 2
    distance = distance + (left_geo[:, 2, :, None] - right_geo[:, 2, None, :]) ** 2
    smooth = factor[:, None, None] * (left_geo[:, 3, :, None] + right_geo[:, 3, None, :])
    return (KERNEL_SCALE / jnp.sqrt(distance + smooth)).astype(jnp.bfloat16)


def tile_products(packed):
    geo_pair, mode_pair, factor, keep_left, keep_right = packed
    kernel = build_kernel(geo_pair[:, 0], geo_pair[:, 1], factor)
    into_left = jnp.einsum(
        "bmq,bpq->bmp", mode_pair[:, 1], kernel, preferred_element_type=jnp.float32
    )
    into_right = jnp.einsum(
        "bmp,bpq->bmq", mode_pair[:, 0], kernel, preferred_element_type=jnp.float32
    )
    into_left = into_left * keep_left[:, None, None]
    into_right = into_right * keep_right[:, None, None]
    return jnp.stack([into_left, into_right], axis=1)


def local(modes, geometry, pair_list, pair_kind):
    group_count = lax.axis_size("grp")
    member_count = lax.axis_size("dev")
    devices = group_count * member_count
    m_rows, panels = modes.shape
    block_panels = P_SIZE
    local_count = panels // block_panels
    slot_count = pair_list.shape[0]
    end_count = 2 * slot_count
    bucket = max(2, (end_count + devices - 1) // devices)
    buf_width = devices * bucket
    end_ids = pair_list.reshape(end_count)
    holder = end_ids // local_count
    local_id = end_ids % local_count
    end_order = jnp.arange(end_count, dtype=jnp.int32)
    earlier = (holder[:, None] == holder[None, :]) & (end_order[None, :] < end_order[:, None])
    bucket_rank = jnp.sum(earlier.astype(jnp.int32), axis=1)
    buffer_slot = holder * bucket + bucket_rank
    placed = buffer_slot[:, None] == jnp.arange(buf_width, dtype=jnp.int32)[None, :]
    request = jnp.sum(jnp.where(placed, local_id[:, None], 0), axis=0)
    wanted = lax.all_to_all(
        request.reshape(devices, bucket), ("grp", "dev"), split_axis=0, concat_axis=0, tiled=True
    ).reshape(buf_width)
    geo_blocks = geometry.reshape(4, local_count, block_panels)
    geo_send = (
        jnp.take(geo_blocks, wanted, axis=1)
        .transpose(1, 0, 2)
        .reshape(devices, bucket, 4, block_panels)
    )
    geo_got = lax.all_to_all(
        geo_send, ("grp", "dev"), split_axis=0, concat_axis=0, tiled=True
    ).reshape(buf_width, 4, block_panels)
    mode_blocks = modes.reshape(m_rows, local_count, block_panels)
    mode_send = jnp.take(mode_blocks, wanted, axis=1).transpose(1, 0, 2)
    mode_got = lax.all_to_all(
        mode_send.reshape(devices, bucket, m_rows, block_panels),
        ("grp", "dev"),
        split_axis=0,
        concat_axis=0,
        tiled=True,
    )
    mode_got = mode_got.reshape(buf_width, m_rows, block_panels)
    group_size = 8
    factor = jnp.where(pair_kind == 2, 0.1, 1.0).astype(jnp.float32)
    keep_left = (pair_kind > 0).astype(jnp.float32)
    keep_right = keep_left * (pair_list[:, 0] != pair_list[:, 1]).astype(jnp.float32)
    step_count = slot_count // group_size
    mine_geo = geo_got[buffer_slot].reshape(step_count, group_size, 2, 4, block_panels)
    mine_modes = mode_got[buffer_slot].reshape(step_count, group_size, 2, m_rows, block_panels)
    contributions = lax.map(
        tile_products,
        (
            mine_geo,
            mine_modes,
            factor.reshape(step_count, group_size),
            keep_left.reshape(step_count, group_size),
            keep_right.reshape(step_count, group_size),
        ),
    )
    contributions = contributions.reshape(end_count, m_rows, block_panels)
    outgoing = (
        jnp.zeros((buf_width, m_rows, block_panels), jnp.float32).at[buffer_slot].set(contributions)
    )
    returned = lax.all_to_all(
        outgoing.reshape(devices, bucket, m_rows, block_panels),
        ("grp", "dev"),
        split_axis=0,
        concat_axis=0,
        tiled=True,
    )
    returned = returned.reshape(buf_width, m_rows, block_panels)
    summed = jax.ops.segment_sum(returned, wanted, num_segments=local_count)
    return summed.transpose(1, 0, 2).reshape(m_rows, panels)


def solution(mesh):
    placed = (
        P(None, ("grp", "dev")),
        P(None, ("grp", "dev")),
        P(("grp", "dev"), None),
        P(("grp", "dev")),
    )
    return jax.shard_map(
        local, mesh=mesh, in_specs=placed, out_specs=P(None, ("grp", "dev")), check_vma=False
    )
```

profile of v0, /device:TPU:1, one launch (start us, length us, event | category | flops | bytes accessed | tf_op | source)
XLA Modules:
  0.0 403.1 jit_solution(14972362282172935394)
XLA Ops:
  2.1 11.5 %all-to-all-start = ((s32[128,1,2]{2,1,0:T(1,128)}), s32[128,1,2]{2,1,0:T(1,128)S(1)}, u32[]{:S(2)}, u32[]{:S(2)}) async-start(s32[128,1,2]{2,1,0:T(1,128)} %bitcast.20), calls=%async_computation | async-start | bytes 131072 | tf_op jit(solution)/shard_map/all_to_all | solution.py:56
  13.6 9.5 %all-to-all-done = s32[128,1,2]{2,1,0:T(1,128)S(1)} async-done(((s32[128,1,2]{2,1,0:T(1,128)}), s32[128,1,2]{2,1,0:T(1,128)S(1)}, u32[]{:S(2)}, u32[]{:S(2)}) %all-to-all-start) | async-done | bytes 1056 | tf_op jit(solution)/shard_map/all_to_all | solution.py:56
  26.0 1.3 broadcast_select_fusion.1
  27.3 4.5 %all-to-all-start.2 = ((f32[128,2,4,256]{3,2,1,0:T(4,128)}), f32[128,2,4,256]{3,2,1,0:T(4,128)S(1)}, u32[]{:S(2)}, u32[]{:S(2)}) async-start(f32[128,2,4,256]{3,2,1,0:T(4,128)} %bitcast.28), calls=%async_computation.2 | async-start | bytes 2097152 | tf_op jit(solution)/shard_map/all_to_all | solution.py:65
  32.0 2.8 gather_fusion
  34.8 4.0 broadcast_select_fusion
  38.8 11.7 %all-to-all-done.2 = f32[128,2,4,256]{3,2,1,0:T(4,128)S(1)} async-done(((f32[128,2,4,256]{3,2,1,0:T(4,128)}), f32[128,2,4,256]{3,2,1,0:T(4,128)S(1)}, u32[]{:S(2)}, u32[]{:S(2)}) %all-to-all-start.2) | async-done | bytes 1048608 | tf_op jit(solution)/shard_map/all_to_all | solution.py:65
  50.5 6.2 %all-to-all-start.1 = ((bf16[128,2,32,256]{3,2,1,0:T(8,128)(2,1)}), bf16[128,2,32,256]{3,2,1,0:T(8,128)(2,1)}, u32[]{:S(2)}, u32[]{:S(2)}) async-start(bf16[128,2,32,256]{3,2,1,0:T(8,128)(2,1)} %bitcast.95), calls=%async_computation.1 | async-start | bytes 8388608 | tf_op jit(solution)/shard_map/all_to_all | solution.py:70
  58.5 50.5 %all-to-all-done.1 = bf16[128,2,32,256]{3,2,1,0:T(8,128)(2,1)} async-done(((bf16[128,2,32,256]{3,2,1,0:T(8,128)(2,1)}), bf16[128,2,32,256]{3,2,1,0:T(8,128)(2,1)}, u32[]{:S(2)}, u32[]{:S(2)}) %all-to-all-start.1) | async-done | bytes 4194336 | tf_op jit(solution)/shard_map/all_to_all | solution.py:70
  109.0 5.0 %gather_fusion.1 = bf16[256,32,256]{2,1,0:T(8,128)(2,1)} fusion(bf16[256,32,256]{2,1,0:T(8,128)(2,1)} %bitcast.25, s32[1024]{0:T(1024)S(1)} %pad_clamp_fusion), kind=kCustom, calls=%fused_computation.1 | custom fusion | bytes 8389632 | tf_op jit(solution)/shard_map/gather | solution.py:84
  113.9 116.7 %while.10 = (s32[]{:T(128)}, f32[16,8,2,32,256]{4,3,2,1,0:T(8,128)}, bf16[16,8,2,32,256]{4,3,2,1,0:T(8,128)(2,1)}, f32[16,8,2,4,256]{4,3,2,1,0:T(4,128)S(1)}, f3...) while((s32[]{:T(128)}, f32[16,8,2,32,256]{4,3,2,1,0:T(8,128)}, ...), condition=%wide.region_3.4_spmd, body=%wide.region_2.3_spmd.sunk | while | flops 81002496 | bytes 3018017 | solution.py:85
  115.0 2.7 fusion.15
  117.7 2.7 fusion.14
  122.3 2.7 fusion.15
  125.0 2.7 fusion.14
  129.6 2.7 fusion.15
  132.3 2.7 fusion.14
  136.9 2.7 fusion.15
  139.6 2.7 fusion.14
  144.1 2.7 fusion.15
  146.8 2.7 fusion.14
  151.4 2.7 fusion.15
  154.1 2.7 fusion.14
  158.7 2.7 fusion.15
  161.4 2.7 fusion.14
  166.0 2.7 fusion.15
  168.7 2.7 fusion.14
  173.3 2.7 fusion.15
  176.0 2.7 fusion.14
  180.6 2.7 fusion.15
  183.3 2.7 fusion.14
  187.9 2.7 fusion.15
  190.6 2.7 fusion.14
  195.2 2.7 fusion.15
  197.9 2.7 fusion.14
  202.5 2.7 fusion.15
  205.2 2.7 fusion.14
  209.8 2.7 fusion.15
  212.5 2.7 fusion.14
  217.1 2.7 fusion.15
  219.8 2.7 fusion.14
  224.4 2.7 fusion.15
  227.1 2.7 fusion.14
  230.6 4.3 %broadcast_in_dim.69 = f32[256,32,256]{2,1,0:T(8,128)} broadcast(f32[]{:T(128)} %constant.75.clone.1), dimensions={} | broadcast | bytes 8388612 | tf_op jit(solution)/shard_map/broadcast_in_dim | solution.py:97
  234.9 37.7 %scatter_fusion = f32[256,32,256]{2,1,0:T(8,128)} fusion(f32[256,32,256]{2,1,0:T(8,128)} %broadcast_in_dim.69, s32[256]{0:T(256)S(1)} %bitcast.103, f32[256,32,256]{2,1,0:T(8,128)} %bitcast.32), kind=kCustom, calls=%fused_computation.4 | custom fusion | bytes 25166848 | tf_op jit(solution)/shard_map/scatter | solution.py:97
  272.6 102.6 %all_to_all.24 = f32[128,2,32,256]{3,2,1,0:T(8,128)} all-to-all(f32[128,2,32,256]{3,2,1,0:T(8,128)} %bitcast.92), channel_id=1, replica_groups=mesh['grp'=8,'dev'=16] {'grp','dev'}, dimensions={0} | all-to-all | bytes 16777216 | tf_op jit(solution)/shard_map/all_to_all | solution.py:99
  375.4 26.1 %scatter_fusion.1 = f32[64,32,256]{2,1,0:T(8,128)S(1)} fusion(f32[64,32,256]{2,1,0:T(8,128)S(1)} %broadcast_in_dim.66, s32[256]{0:T(256)S(1)} %reshape.323, f32[256,32,256]{2,1,0:T(8,128)} %bitcast.93), kind=kCustom, calls=%fused_computation.5 | custom fusion | flops 2097152 | bytes 25166848 | tf_op jit(solution)/shard_map/scatter-add | solution.py:107
  401.5 1.5 copy.38
  (163 shorter events, 37.4 us)
Async XLA Ops:
  0.0 24.7 %copy-start = (f32[4,16384]{1,0:T(4,128)S(1)}, f32[4,16384]{1,0:T(4,128)}, u32[]{:S(2)}) copy-start(f32[4,16384]{1,0:T(4,128)} %param.7) | copy-start | bytes 786436
  2.1 21.0 %all-to-all-start = ((s32[128,1,2]{2,1,0:T(1,128)}), s32[128,1,2]{2,1,0:T(1,128)S(1)}, u32[]{:S(2)}, u32[]{:S(2)}) async-start(s32[128,1,2]{2,1,0:T(1,128)} %bitcast.20), calls=%async_computation | async-start | bytes 131072 | tf_op jit(solution)/shard_map/all_to_all | solution.py:56
  26.0 5.9 %copy-start.1 = (bf16[32,16384]{1,0:T(8,128)(2,1)S(1)}, bf16[32,16384]{1,0:T(8,128)(2,1)}, u32[]{:S(2)}) copy-start(bf16[32,16384]{1,0:T(8,128)(2,1)} %param.6) | copy-start | bytes 3145732
  27.3 23.2 %all-to-all-start.2 = ((f32[128,2,4,256]{3,2,1,0:T(4,128)}), f32[128,2,4,256]{3,2,1,0:T(4,128)S(1)}, u32[]{:S(2)}, u32[]{:S(2)}) async-start(f32[128,2,4,256]{3,2,1,0:T(4,128)} %bitcast.28), calls=%async_computation.2 | async-start | bytes 2097152 | tf_op jit(solution)/shard_map/all_to_all | solution.py:65
  50.5 6.3 %copy-start.2 = (s32[128,2]{0,1:T(2,128)S(1)}, s32[128,2]{0,1:T(2,128)}, u32[]{:S(2)}) copy-start(s32[128,2]{0,1:T(2,128)} %param.8) | copy-start | bytes 3076
  50.5 6.3 %copy-start.3 = (s32[128]{0:T(128)S(1)}, s32[128]{0:T(128)}, u32[]{:S(2)}) copy-start(s32[128]{0:T(128)} %param.9) | copy-start | bytes 1540
  50.5 58.4 %all-to-all-start.1 = ((bf16[128,2,32,256]{3,2,1,0:T(8,128)(2,1)}), bf16[128,2,32,256]{3,2,1,0:T(8,128)(2,1)}, u32[]{:S(2)}, u32[]{:S(2)}) async-start(bf16[128,2,32,256]{3,2,1,0:T(8,128)(2,1)} %bitcast.95), calls=%async_computation.1 | async-start | bytes 8388608 | tf_op jit(solution)/shard_map/all_to_all | solution.py:70
where the time goes:
time: 405 us; the launch traced here: 403 us
  blocking collectives  103 us (25%)
  matrix products  85.8 us (21%)
  local copies, waits for them, and re-layouts  73.7 us (18%)
  waiting for transfers between devices  71.7 us (18%)
  other arithmetic  46.4 us (11%)
  starting transfers between devices  22.2 us (5%)
    all_to_all x1, blocking collectives, local(): lax.all_to_all(outgoing.reshape(devices, bucket, m_rows, block_panels), (...  103 us
    all_to_all x1, waiting for transfers between devices, local(): lax.all_to_all(mode_send.reshape(devices, bucket, m_rows, block_panels),...  50.5 us
    dot_general x16, matrix products, tile_products(): jnp.einsum('bmq,bpq->bmp', mode_pair[:, 1], kernel, preferred_element_typ...  43.1 us
    dot_general x16, matrix products, tile_products(): jnp.einsum('bmp,bpq->bmq', mode_pair[:, 0], kernel, preferred_element_typ...  42.7 us
    scatter x1, local copies, waits for them, and re-layouts, local(): jnp.zeros((buf_width, m_rows, block_panels), jnp.float32).at[buffer_slot]  37.7 us
    scatter-add x1, other arithmetic, local(): summed = jax.ops.segment_sum(returned, wanted, num_segments=local_count)  26.1 us
    squeeze x16, local copies, waits for them, and re-layouts, local(): lax.map(tile_products, (mine_geo, mine_modes, factor.reshape(step_count,...  15.6 us
    dynamic_update_slice x16, other arithmetic, local(): lax.map(tile_products, (mine_geo, mine_modes, factor.reshape(step_count,...  13.7 us
  transfers between devices with their start and end apart: 3, of which 3 were waited for; matrix products, arithmetic and copies ran while one was open for 2% of the time, Pallas kernels for 0%

commit v1 on v0

v1 whole, which is shorter than its diff:
```python
import functools
import math

import jax
import jax.numpy as jnp
from jax import lax
from jax.experimental import pallas as pl
from jax.experimental.pallas import tpu as pltpu
from jax.sharding import PartitionSpec as P

P_SIZE = 256
MODES = 32
KEY = 16
FOUR_PI = 4.0 * math.pi
MESH = pl.DeviceIdType.MESH


def split_two(value):
    high = value.astype(jnp.bfloat16)
    low = (value - high.astype(jnp.float32)).astype(jnp.bfloat16)
    return high, low


def split_three(value):
    high = value.astype(jnp.bfloat16)
    rest = value - high.astype(jnp.float32)
    mid = rest.astype(jnp.bfloat16)
    low = (rest - mid.astype(jnp.float32)).astype(jnp.bfloat16)
    return high, mid, low


def exchange_kernel(
    groups, members, side,
    code_ref, request_ref, modes_ref, geo_ref,
    back_ref, asked_ref,
    asked_smem, mode_blocks, geo_blocks, geo_stage, geo_got, mode_stage, mode_got, mode_back,
    left_xyz, right_xyz, left_norm, right_norm,
    send_sems, recv_sems, local_sem,
):
    devices = groups * members
    others = devices - 1
    grp = lax.axis_index("grp")
    dev = lax.axis_index("dev")
    me = grp * members + dev
    halves = groups // 2

    def partner_of(step):
        shift = (step * 45) % devices
        dg, dv = shift // members, shift % members
        y = (grp // 2 + dg // 2) % halves
        core = (grp + dg) % 2
        x = (dev // side + dv // side) % side
        z = (dev + dv) % side
        return y * 2 + core, x * side + z

    barrier = pltpu.get_barrier_semaphore()

    @pl.loop(1, devices)
    def _(step):
        pl.semaphore_signal(barrier, inc=1, device_id=partner_of(step), device_id_type=MESH)

    for cluster in range(mode_blocks.shape[0]):
        mode_blocks[cluster] = modes_ref[:, cluster * P_SIZE : (cluster + 1) * P_SIZE]
        geo_blocks[cluster] = geo_ref[:, cluster * P_SIZE : (cluster + 1) * P_SIZE]

    pl.semaphore_wait(barrier, others)

    def send(source, target, which, place):
        pltpu.make_async_remote_copy(
            src_ref=source, dst_ref=target,
            send_sem=send_sems.at[which], recv_sem=recv_sems.at[which],
            device_id=place, device_id_type=MESH,
        ).start()

    def drain(source, target, which):
        return pltpu.make_async_remote_copy(
            src_ref=source, dst_ref=target,
            send_sem=send_sems.at[which], recv_sem=recv_sems.at[which],
            device_id=(grp, dev), device_id_type=MESH,
        )

    @pl.loop(1, devices)
    def _(step):
        to_grp, to_dev = partner_of(step)
        to = to_grp * members + to_dev
        send(request_ref.at[to], asked_ref.at[me], 0, (to_grp, to_dev))

    asked_ref[me] = request_ref[me]
    requests = drain(request_ref.at[pl.ds(0, others)], asked_ref.at[pl.ds(0, others)], 0)
    requests.wait_recv()
    local = pltpu.make_async_copy(asked_ref, asked_smem, local_sem)
    local.start()
    local.wait()

    def wanted(to, rank):
        return asked_smem[to, 0, rank] & 63

    @pl.loop(1, devices)
    def _(step):
        to_grp, to_dev = partner_of(step)
        to = to_grp * members + to_dev
        geo_stage[to, 0:4] = geo_blocks[wanted(to, 0)]
        geo_stage[to, 4:8] = geo_blocks[wanted(to, 1)]
        send(geo_stage.at[to], geo_got.at[me], 1, (to_grp, to_dev))

    @pl.loop(1, devices)
    def _(step):
        to_grp, to_dev = partner_of(step)
        to = to_grp * members + to_dev
        mode_stage[2 * to] = mode_blocks[wanted(to, 0)]
        mode_stage[2 * to + 1] = mode_blocks[wanted(to, 1)]
        send(mode_stage.at[pl.ds(2 * to, 2)], mode_got.at[pl.ds(2 * me, 2)], 2, (to_grp, to_dev))

    geo_got[me, 0:4] = geo_blocks[wanted(me, 0)]
    geo_got[me, 4:8] = geo_blocks[wanted(me, 1)]
    mode_got[2 * me] = mode_blocks[wanted(me, 0)]
    mode_got[2 * me + 1] = mode_blocks[wanted(me, 1)]
    geos = drain(geo_stage.at[pl.ds(0, others)], geo_got.at[pl.ds(0, others)], 1)
    geos.wait_recv()

    one = jnp.ones((1, P_SIZE), jnp.bfloat16)
    rest = jnp.zeros((KEY - 6, P_SIZE), jnp.bfloat16)
    pad = jnp.zeros((KEY - 12, P_SIZE), jnp.bfloat16)

    @pl.loop(0, devices)
    def _(source):
        block = geo_got[source]
        for rank in range(2):
            slot = 2 * source + rank
            xyz = block[4 * rank : 4 * rank + 3] * FOUR_PI
            area = block[4 * rank + 3 : 4 * rank + 4] * (FOUR_PI * FOUR_PI)
            high, low = split_two(xyz)
            high32, low32 = high.astype(jnp.float32), low.astype(jnp.float32)
            twice_high = (high32 * -2.0).astype(jnp.bfloat16)
            twice_low = (low32 * -2.0).astype(jnp.bfloat16)
            left_xyz[slot] = jnp.concatenate([twice_high, twice_high, twice_low, twice_low, pad], axis=0)
            right_xyz[slot] = jnp.concatenate([high, low, high, low, pad], axis=0)
            whole = high32 + low32
            square = whole * whole
            norm = square[0:1] + square[1:2] + square[2:3]
            for kind, factor in enumerate((1.0, 0.1)):
                a, b, c = split_three(norm + area * factor)
                left_norm[kind * 2 * devices + slot] = jnp.concatenate([a, b, c, one, one, one, rest], axis=0)
                right_norm[kind * 2 * devices + slot] = jnp.concatenate([one, one, one, a, b, c, rest], axis=0)

    gots = drain(mode_stage.at[pl.ds(0, 2 * others)], mode_got.at[pl.ds(0, 2 * others)], 2)
    gots.wait_recv()

    def product(slot):
        code = code_ref[slot]
        other = (code >> 6) & 255
        kind = ((code >> 14) & 1) * (2 * devices)
        keep = ((code >> 15) & 1).astype(jnp.float32)
        left = jnp.concatenate([left_xyz[other], left_norm[kind + other]], axis=0)
        right = jnp.concatenate([right_xyz[slot], right_norm[kind + slot]], axis=0)
        squared = lax.dot_general(
            left, right, (((0,), (0,)), ((), ())), preferred_element_type=jnp.float32
        )
        tile = lax.rsqrt(squared).astype(jnp.bfloat16)
        out = jnp.dot(mode_got[other], tile, preferred_element_type=jnp.float32)
        mode_back[slot] = (out * keep).astype(jnp.bfloat16)

    @pl.loop(1, devices)
    def _(step):
        to_grp, to_dev = partner_of(step)
        to = to_grp * members + to_dev
        product(2 * to)
        product(2 * to + 1)
        send(mode_back.at[pl.ds(2 * to, 2)], back_ref.at[pl.ds(2 * me, 2)], 3, (to_grp, to_dev))

    product(2 * me)
    product(2 * me + 1)
    own = pltpu.make_async_copy(
        mode_back.at[pl.ds(2 * me, 2)], back_ref.at[pl.ds(2 * me, 2)], local_sem
    )
    own.start()
    own.wait()
    backs = drain(mode_back.at[pl.ds(0, 2 * others)], back_ref.at[pl.ds(0, 2 * others)], 3)
    backs.wait_recv()
    requests.wait_send()
    geos.wait_send()
    gots.wait_send()
    backs.wait_send()


def sum_kernel(group, asked_ref, back_ref, out_ref):
    step = pl.program_id(0)

    @pl.when(step == 0)
    def _():
        out_ref[...] = jnp.zeros_like(out_ref)

    for index in range(group):
        slot = step * group + index
        cluster = asked_ref[slot // 2, 0, slot % 2] & 63
        place = pl.ds(pl.multiple_of(cluster * P_SIZE, P_SIZE), P_SIZE)
        out_ref[:, place] += back_ref[index].astype(jnp.float32)


def local(modes, geometry, pair_list, pair_kind):
    groups = lax.axis_size("grp")
    members = lax.axis_size("dev")
    devices = groups * members
    side = math.isqrt(members)
    local_count = modes.shape[1] // P_SIZE
    slots = pair_list.shape[0]
    ends = 2 * slots

    end_ids = pair_list.reshape(ends)
    holder = end_ids // local_count
    order = jnp.arange(ends, dtype=jnp.int32)
    earlier = (holder[:, None] == holder[None, :]) & (order[None, :] < order[:, None])
    place = 2 * holder + jnp.any(earlier, axis=1).astype(jnp.int32)
    other = place.reshape(slots, 2)[:, ::-1].reshape(ends)
    live = pair_kind > 0
    keep = jnp.stack([live, live & (pair_list[:, 0] != pair_list[:, 1])], axis=1).reshape(ends)
    admissible = jnp.repeat(pair_kind == 2, 2)
    code = (
        end_ids % local_count
        + 64 * other
        + 16384 * admissible.astype(jnp.int32)
        + 32768 * keep.astype(jnp.int32)
    )
    code = jnp.sum(jnp.where(place[:, None] == order[None, :], code[:, None], 0), axis=0)
    request = jnp.pad(code.reshape(devices, 1, 2), ((0, 0), (0, 0), (0, 126)))

    vmem = pl.BlockSpec(memory_space=pltpu.VMEM)
    back, asked = pl.pallas_call(
        functools.partial(exchange_kernel, groups, members, side),
        out_shape=[
            jax.ShapeDtypeStruct((ends, MODES, P_SIZE), jnp.bfloat16),
            jax.ShapeDtypeStruct((devices, 1, 128), jnp.int32),
        ],
        in_specs=[pl.BlockSpec(memory_space=pltpu.SMEM), vmem, vmem, vmem],
        out_specs=[pl.BlockSpec(memory_space=pl.ANY), vmem],
        scratch_shapes=[
            pltpu.SMEM((devices, 1, 128), jnp.int32),
            pltpu.VMEM((local_count, MODES, P_SIZE), jnp.bfloat16),
            pltpu.VMEM((local_count, 4, P_SIZE), jnp.float32),
            pltpu.VMEM((devices, 8, P_SIZE), jnp.float32),
            pltpu.VMEM((devices, 8, P_SIZE), jnp.float32),
            pltpu.VMEM((ends, MODES, P_SIZE), jnp.bfloat16),
            pltpu.VMEM((ends, MODES, P_SIZE), jnp.bfloat16),
            pltpu.VMEM((ends, MODES, P_SIZE), jnp.bfloat16),
            pltpu.VMEM((ends, KEY, P_SIZE), jnp.bfloat16),
            pltpu.VMEM((ends, KEY, P_SIZE), jnp.bfloat16),
            pltpu.VMEM((2 * ends, KEY, P_SIZE), jnp.bfloat16),
            pltpu.VMEM((2 * ends, KEY, P_SIZE), jnp.bfloat16),
            pltpu.SemaphoreType.DMA((4,)),
            pltpu.SemaphoreType.DMA((4,)),
            pltpu.SemaphoreType.DMA,
        ],
        compiler_params=pltpu.CompilerParams(
            collective_id=0, has_side_effects=True, vmem_limit_bytes=48 * 1024 * 1024
        ),
    )(code, request, modes, geometry)

    group = 16
    return pl.pallas_call(
        functools.partial(sum_kernel, group),
        grid=(ends // group,),
        out_shape=jax.ShapeDtypeStruct((MODES, local_count * P_SIZE), jnp.float32),
        in_specs=[
            pl.BlockSpec(memory_space=pltpu.SMEM),
            pl.BlockSpec((group, MODES, P_SIZE), lambda step: (step, 0, 0)),
        ],
        out_specs=pl.BlockSpec((MODES, local_count * P_SIZE), lambda step: (0, 0)),
        compiler_params=pltpu.CompilerParams(vmem_limit_bytes=24 * 1024 * 1024),
    )(asked, back)


def solution(mesh):
    placed = (
        P(None, ("grp", "dev")),
        P(None, ("grp", "dev")),
        P(("grp", "dev"), None),
        P(("grp", "dev")),
    )
    return jax.shard_map(
        local, mesh=mesh, in_specs=placed, out_specs=P(None, ("grp", "dev")), check_vma=False
    )
```

time: 405 us -> 177 us (0.44)
  Pallas kernels: 0 us -> 169 us
  blocking collectives: 103 us -> 0 us
  matrix products: 85.8 us -> 0 us
  waiting for transfers between devices: 71.7 us -> 0 us
  local copies, waits for them, and re-layouts: 73.7 us -> 4.28 us
  other arithmetic: 46.4 us -> 2.55 us
  starting transfers between devices: 22.2 us -> 0 us
    pallas_call x0 -> x2, Pallas kernels: none -> 169 us  [the longest x1 164 us: local(): pl.pallas_call(functools.partial(exchange_kernel, groups, members, side),...]
    all_to_all x1 -> x0, blocking collectives: 103 us -> none  [local(): lax.all_to_all(outgoing.reshape(devices, bucket, m_rows, block_panels), (...]
    dot_general x32 -> x0, matrix products: 85.8 us -> none  [the longest x16 43.1 us: tile_products(): jnp.einsum('bmq,bpq->bmp', mode_pair[:, 1], kernel, preferred_element_typ...]
    all_to_all x3 -> x0, waiting for transfers between devices: 71.7 us -> none  [the longest x1 50.5 us: local(): lax.all_to_all(mode_send.reshape(devices, bucket, m_rows, block_panels),...]
    scatter x1 -> x0, local copies, waits for them, and re-layouts: 37.7 us -> none  [local(): jnp.zeros((buf_width, m_rows, block_panels), jnp.float32).at[buffer_slot]]
    scatter-add x1 -> x0, other arithmetic: 26.1 us -> none  [local(): summed = jax.ops.segment_sum(returned, wanted, num_segments=local_count)]
    all_to_all x3 -> x0, starting transfers between devices: 22.2 us -> none  [the longest x1 11.5 us: local(): lax.all_to_all(request.reshape(devices, bucket), ('grp', 'dev'), split_ax...]
    squeeze x32 -> x0, local copies, waits for them, and re-layouts: 15.7 us -> none  [the longest x16 15.6 us: local(): lax.map(tile_products, (mine_geo, mine_modes, factor.reshape(step_count,...]
  transfers between devices with their start and end apart: 3 -> 0, of which waited for: 3 -> 0; matrix products, arithmetic and copies ran while one was open for 2% -> 0% of each run, Pallas kernels for 0% -> 0%
where the time goes in v1:
time: 177 us; the launch traced here: 176 us
  Pallas kernels  169 us (95%)
  local copies, waits for them, and re-layouts  4.28 us (2%)
  other arithmetic  2.55 us (1%)
    pallas_call x1, Pallas kernels, local(): pl.pallas_call(functools.partial(exchange_kernel, groups, members, side),...  164 us
    pallas_call x1, Pallas kernels, local(): pl.pallas_call(functools.partial(sum_kernel, group), grid=(ends // group,...  5.65 us

profile of v1, /device:TPU:1, one launch (start us, length us, event | category | flops | bytes accessed | tf_op | source)
XLA Modules:
  0.0 176.4 jit_solution(7739578677474633524)
XLA Ops:
  0.0 0.7 compare_select_fusion
  0.7 0.7 broadcast_compare_fusion
  1.3 0.8 compare_bitcast_fusion
  2.1 0.1 copy.34
  2.3 0.1 copy.32
  2.4 0.1 mul.53
  2.5 0.1 broadcast_in_dim.10
  2.6 0.2 mul.50
  2.8 0.8 copy.26
  3.6 0.1 reshape.131
  3.7 0.2 fusion.1
  3.9 0.1 reshape.133
  4.1 0.1 fusion.4
  4.1 0.1 rev.3
  4.2 0.1 mul.47
  4.4 0.1 select_reduce_fusion.code_ref
  4.5 0.1 reshape.132
  4.7 0.0 copy-start
  4.7 1.2 copy-done
  6.0 0.0 copy-start.1
  6.0 0.9 copy-done.1
  6.9 163.8 %shard_map.46 = (bf16[256,32,256]{2,1,0:T(8,128)(2,1)S(1)}, s32[128,1,128]{2,1,0:T(1,128)S(1)}) custom-call(s32[256]{0:T(256)S(1)} %select_reduce_fusion.code_ref, s32[128,1,128]{2,1,0:T(1,128)S(1)} %pad.4.request_ref, bf16[32,16384]{1,0:T(8,128)(2,1)S(1)} %copy-done, f32[4,16384]{1,0:T(4,128)S(1)} %copy-done.1), custom_call_target="tpu_custom_call" | custom-call | tf_op jit(solution)/shard_map/pallas_call | solution.py:228
  170.7 5.7 %shard_map.47 = f32[32,16384]{1,0:T(8,128)} custom-call(s32[128,1,128]{2,1,0:T(1,128)S(1)} %get-tuple-element.7.asked_ref, bf16[256,32,256]{2,1,0:T(8,128)(2,1)S(1)} %get-tuple-element.8.back_ref), custom_call_target="tpu_custom_call" | custom-call | tf_op jit(solution)/shard_map/pallas_call | solution.py:259
  (7 shorter events, 0.1 us)
Async XLA Ops:
  4.7 1.2 copy-start
  6.0 0.9 copy-start.1

commit v2 on v1

v2 whole, which is shorter than its diff:
```python
import functools
import math

import jax
import jax.numpy as jnp
from jax import lax
from jax.experimental import pallas as pl
from jax.experimental.pallas import tpu as pltpu
from jax.sharding import PartitionSpec as P

P_SIZE = 256
MODES = 32
FOUR_PI = 4.0 * math.pi
MESH = pl.DeviceIdType.MESH


def thirds(value):
    high = value.astype(jnp.bfloat16).astype(jnp.float32)
    rest = value - high
    mid = rest.astype(jnp.bfloat16).astype(jnp.float32)
    return high, mid, rest - mid


def column(row):
    count = row.shape[1]
    down = lax.broadcasted_iota(jnp.int32, (count, count), 0)
    across = lax.broadcasted_iota(jnp.int32, (count, count), 1)
    return jnp.sum(jnp.where(down == across, row, 0), axis=1, keepdims=True)


def slot_table(pair_ids, kinds, local_count):
    slots = pair_ids.shape[1]
    ends = 2 * slots
    left, right = pair_ids[0:1], pair_ids[1:2]
    ids = jnp.concatenate([left, right], axis=1)
    holder = lax.div(ids, local_count)
    down = lax.broadcasted_iota(jnp.int32, (ends, ends), 0)
    across = lax.broadcasted_iota(jnp.int32, (ends, ends), 1)
    earlier = (column(holder) == holder) & (down < across)
    rank = jnp.sum(jnp.where(earlier, 1, 0), axis=0, keepdims=True)
    place = 2 * holder + rank
    other = jnp.concatenate([place[:, slots:], place[:, :slots]], axis=1)
    live = jnp.where(kinds > 0, 1, 0)
    twice = jnp.where(left != right, live, 0)
    keep = jnp.concatenate([live, twice], axis=1)
    admissible = jnp.where(kinds == 2, 1, 0)
    admissible = jnp.concatenate([admissible, admissible], axis=1)
    code = lax.rem(ids, local_count) + 64 * other + 16384 * admissible + 32768 * keep
    return jnp.sum(jnp.where(column(place) == across, column(code), 0), axis=0, keepdims=True)


def exchange_kernel(
    groups, members, side, ahead,
    pair_ref, kind_ref, modes_ref, geo_ref,
    back_ref, wanted_ref,
    code_vmem, code_smem, asked_vmem, asked_smem,
    mode_blocks, geo_blocks, geo_stage, geo_got, mode_stage, mode_got, mode_back, tiles,
    send_sems, recv_sems, local_sem,
):
    devices = groups * members
    others = devices - 1
    local_count = mode_blocks.shape[0]
    grp = lax.axis_index("grp")
    dev = lax.axis_index("dev")
    me = grp * members + dev
    member_bits = members.bit_length() - 1
    side_bits = side.bit_length() - 1

    def partner_of(step):
        shift = (step * 45) & (devices - 1)
        dg, dv = shift >> member_bits, shift & (members - 1)
        y = ((grp >> 1) + (dg >> 1)) & (groups // 2 - 1)
        core = (grp + dg) & 1
        x = ((dev >> side_bits) + (dv >> side_bits)) & (side - 1)
        z = (dev + dv) & (side - 1)
        return y * 2 + core, x * side + z

    barrier = pltpu.get_barrier_semaphore()

    @pl.loop(1, devices)
    def _(step):
        pl.semaphore_signal(barrier, inc=1, device_id=partner_of(step), device_id_type=MESH)

    code_vmem[...] = slot_table(pair_ref[...], kind_ref[...], local_count)
    local = pltpu.make_async_copy(code_vmem, code_smem, local_sem)
    local.start()
    for cluster in range(local_count):
        mode_blocks[cluster] = modes_ref[:, cluster * P_SIZE : (cluster + 1) * P_SIZE]
        geo_blocks[cluster] = geo_ref[:, cluster * P_SIZE : (cluster + 1) * P_SIZE]
    local.wait()

    pl.semaphore_wait(barrier, others)

    def send(source, target, which, place):
        pltpu.make_async_remote_copy(
            src_ref=source, dst_ref=target,
            send_sem=send_sems.at[which], recv_sem=recv_sems.at[which],
            device_id=place, device_id_type=MESH,
        ).start()

    def drain(source, target, which):
        return pltpu.make_async_remote_copy(
            src_ref=source, dst_ref=target,
            send_sem=send_sems.at[which], recv_sem=recv_sems.at[which],
            device_id=(grp, dev), device_id_type=MESH,
        )

    @pl.loop(1, devices)
    def _(step):
        send(code_vmem, asked_vmem.at[me], 0, partner_of(step))

    asked_vmem[me] = code_vmem[...]
    requests = drain(asked_vmem.at[pl.ds(0, others)], asked_vmem.at[pl.ds(0, others)], 0)
    requests.wait_recv()
    local = pltpu.make_async_copy(asked_vmem, asked_smem, local_sem)
    local.start()
    local.wait()

    def wanted(to, rank):
        return asked_smem[to, 0, 2 * me + rank] & 63

    @pl.loop(1, devices)
    def _(step):
        to_grp, to_dev = partner_of(step)
        to = to_grp * members + to_dev
        for rank in range(2):
            cluster = wanted(to, rank)
            wanted_ref[2 * to + rank] = cluster
            geo_stage[to, 4 * rank : 4 * rank + 4] = geo_blocks[cluster]
        send(geo_stage.at[to], geo_got.at[me], 1, (to_grp, to_dev))

    @pl.loop(1, devices)
    def _(step):
        to_grp, to_dev = partner_of(step)
        to = to_grp * members + to_dev
        for rank in range(2):
            mode_stage[2 * to + rank] = mode_blocks[wanted(to, rank)]
        send(mode_stage.at[pl.ds(2 * to, 2)], mode_got.at[pl.ds(2 * me, 2)], 2, (to_grp, to_dev))

    for rank in range(2):
        cluster = wanted(me, rank)
        wanted_ref[2 * me + rank] = cluster
        geo_got[me, 4 * rank : 4 * rank + 4] = geo_blocks[cluster]
        mode_got[2 * me + rank] = mode_blocks[cluster]
    geos = drain(geo_stage.at[pl.ds(0, others)], geo_got.at[pl.ds(0, others)], 1)
    geos.wait_recv()

    row = lax.broadcasted_iota(jnp.int32, (8, P_SIZE), 0)
    scale = jnp.where(row < 3, FOUR_PI, FOUR_PI * FOUR_PI)

    def prepared(block, factor):
        block = block * scale
        square = block * block
        norm = square[0:1] + square[1:2] + square[2:3] + block[3:4] * factor
        return block, norm

    def tile_of(to, rank):
        code = code_smem[0, 2 * to + rank]
        other = (code >> 6) & 255
        factor = jnp.where((code & 16384) != 0, jnp.float32(0.1), jnp.float32(1.0))
        mine = geo_got[to]
        theirs = geo_got[other >> 1]
        if rank == 1:
            mine = pltpu.roll(mine, 4, 0)
        theirs = jnp.where((other & 1) == 1, pltpu.roll(theirs, 4, 0), theirs)
        block, norm = prepared(mine, factor)
        right = jnp.where(row < 3, block, jnp.where(row == 3, norm, jnp.where(row == 4, 1.0, 0.0)))
        block, norm = prepared(theirs, factor)
        left = jnp.where(
            row < 3, -2.0 * block, jnp.where(row == 3, 1.0, jnp.where(row == 4, norm, 0.0))
        )
        a, b, c = thirds(left)
        left = jnp.concatenate([a, b, a, b, c, a], axis=0).astype(jnp.bfloat16)
        a, b, c = thirds(right)
        right = jnp.concatenate([a, a, b, b, a, c], axis=0).astype(jnp.bfloat16)
        squared = lax.dot_general(
            left, right, (((0,), (0,)), ((), ())), preferred_element_type=jnp.float32
        )
        return lax.rsqrt(squared).astype(jnp.bfloat16)

    @pl.loop(1, ahead)
    def _(step):
        to_grp, to_dev = partner_of(step)
        to = to_grp * members + to_dev
        for rank in range(2):
            tiles[2 * step + rank] = tile_of(to, rank)

    gots = drain(mode_stage.at[pl.ds(0, 2 * others)], mode_got.at[pl.ds(0, 2 * others)], 2)
    gots.wait_recv()

    def product(to, rank, tile):
        code = code_smem[0, 2 * to + rank]
        keep = ((code >> 15) & 1).astype(jnp.float32)
        out = jnp.dot(mode_got[(code >> 6) & 255], tile, preferred_element_type=jnp.float32)
        mode_back[2 * to + rank] = (out * keep).astype(jnp.bfloat16)

    def give_back(to, place):
        send(mode_back.at[pl.ds(2 * to, 2)], back_ref.at[pl.ds(2 * me, 2)], 3, place)

    @pl.loop(1, ahead)
    def _(step):
        to_grp, to_dev = partner_of(step)
        to = to_grp * members + to_dev
        for rank in range(2):
            product(to, rank, tiles[2 * step + rank])
        give_back(to, (to_grp, to_dev))

    @pl.loop(ahead, devices)
    def _(step):
        to_grp, to_dev = partner_of(step)
        to = to_grp * members + to_dev
        for rank in range(2):
            product(to, rank, tile_of(to, rank))
        give_back(to, (to_grp, to_dev))

    for rank in range(2):
        product(me, rank, tile_of(me, rank))
    own = pltpu.make_async_copy(
        mode_back.at[pl.ds(2 * me, 2)], back_ref.at[pl.ds(2 * me, 2)], local_sem
    )
    own.start()
    own.wait()
    backs = drain(mode_back.at[pl.ds(0, 2 * others)], back_ref.at[pl.ds(0, 2 * others)], 3)
    backs.wait_recv()
    requests.wait_send()
    geos.wait_send()
    gots.wait_send()
    backs.wait_send()


def sum_kernel(group, wanted_ref, back_ref, out_ref):
    step = pl.program_id(0)

    @pl.when(step == 0)
    def _():
        out_ref[...] = jnp.zeros_like(out_ref)

    for index in range(group):
        cluster = wanted_ref[step * group + index]
        place = pl.ds(pl.multiple_of(cluster * P_SIZE, P_SIZE), P_SIZE)
        out_ref[:, place] += back_ref[index].astype(jnp.float32)


def local(modes, geometry, pair_list, pair_kind):
    groups = lax.axis_size("grp")
    members = lax.axis_size("dev")
    devices = groups * members
    side = math.isqrt(members)
    local_count = modes.shape[1] // P_SIZE
    slots = pair_list.shape[0]
    ends = 2 * slots
    ahead = devices * 3 // 4

    vmem = pl.BlockSpec(memory_space=pltpu.VMEM)
    smem = pl.BlockSpec(memory_space=pltpu.SMEM)
    back, wanted = pl.pallas_call(
        functools.partial(exchange_kernel, groups, members, side, ahead),
        out_shape=[
            jax.ShapeDtypeStruct((ends, MODES, P_SIZE), jnp.bfloat16),
            jax.ShapeDtypeStruct((ends,), jnp.int32),
        ],
        in_specs=[vmem, vmem, vmem, vmem],
        out_specs=[pl.BlockSpec(memory_space=pl.ANY), smem],
        scratch_shapes=[
            pltpu.VMEM((1, ends), jnp.int32),
            pltpu.SMEM((1, ends), jnp.int32),
            pltpu.VMEM((devices, 1, ends), jnp.int32),
            pltpu.SMEM((devices, 1, ends), jnp.int32),
            pltpu.VMEM((local_count, MODES, P_SIZE), jnp.bfloat16),
            pltpu.VMEM((local_count, 4, P_SIZE), jnp.float32),
            pltpu.VMEM((devices, 8, P_SIZE), jnp.float32),
            pltpu.VMEM((devices, 8, P_SIZE), jnp.float32),
            pltpu.VMEM((ends, MODES, P_SIZE), jnp.bfloat16),
            pltpu.VMEM((ends, MODES, P_SIZE), jnp.bfloat16),
            pltpu.VMEM((ends, MODES, P_SIZE), jnp.bfloat16),
            pltpu.VMEM((2 * ahead, P_SIZE, P_SIZE), jnp.bfloat16),
            pltpu.SemaphoreType.DMA((4,)),
            pltpu.SemaphoreType.DMA((4,)),
            pltpu.SemaphoreType.DMA,
        ],
        compiler_params=pltpu.CompilerParams(
            collective_id=0, has_side_effects=True, vmem_limit_bytes=56 * 1024 * 1024
        ),
    )(pair_list.T, pair_kind.reshape(1, slots), modes, geometry)

    group = 16
    return pl.pallas_call(
        functools.partial(sum_kernel, group),
        grid=(ends // group,),
        out_shape=jax.ShapeDtypeStruct((MODES, local_count * P_SIZE), jnp.float32),
        in_specs=[
            smem,
            pl.BlockSpec((group, MODES, P_SIZE), lambda step: (step, 0, 0)),
        ],
        out_specs=pl.BlockSpec((MODES, local_count * P_SIZE), lambda step: (0, 0)),
        compiler_params=pltpu.CompilerParams(vmem_limit_bytes=24 * 1024 * 1024),
    )(wanted, back)


def solution(mesh):
    placed = (
        P(None, ("grp", "dev")),
        P(None, ("grp", "dev")),
        P(("grp", "dev"), None),
        P(("grp", "dev")),
    )
    return jax.shard_map(
        local, mesh=mesh, in_specs=placed, out_specs=P(None, ("grp", "dev")), check_vma=False
    )
```

time: 177 us -> 139 us (0.79)
  Pallas kernels: 169 us -> 136 us
  other arithmetic: 2.55 us -> 0 us
    pallas_call x1, Pallas kernels: 164 us -> 132 us  [local(): pl.pallas_call(functools.partial(exchange_kernel, groups, members, side,...]
    pallas_call x1, Pallas kernels: 5.65 us -> 3.63 us  [local(): pl.pallas_call(functools.partial(sum_kernel, group), grid=(ends // group,...]
where the time goes in v2:
time: 139 us
  Pallas kernels  136 us (98%)
  local copies, waits for them, and re-layouts  2.86 us (2%)
    pallas_call x1, Pallas kernels, local(): pl.pallas_call(functools.partial(exchange_kernel, groups, members, side,...  132 us
    pallas_call x1, Pallas kernels, local(): pl.pallas_call(functools.partial(sum_kernel, group), grid=(ends // group,...  3.63 us
    unnamed x4, local copies, waits for them, and re-layouts  2.86 us

profile of v2, /device:TPU:1, one launch (start us, length us, event | category | flops | bytes accessed | tf_op | source)
XLA Modules:
  0.0 138.7 jit_solution(5782085948471995628)
XLA Ops:
  0.0 132.2 %shard_map.46 = (bf16[256,32,256]{2,1,0:T(8,128)(2,1)}, s32[256]{0:T(256)}) custom-call(s32[2,128]{1,0:T(2,128)} %bitcast.2, s32[1,128]{1,0:T(1,128)} %bitcast.3, bf16[32,16384]{1,0:T(8,128)(2,1)} %modes_ref.1, f32[4,16384]{1,0:T(4,128)} %geo_ref.1), custom_call_target="tpu_custom_call" | custom-call | tf_op jit(solution)/shard_map/pallas_call | solution.py:256
  132.2 0.0 copy-start
  132.2 2.2 %copy-done = bf16[256,32,256]{2,1,0:T(8,128)(2,1)S(1)} copy-done((bf16[256,32,256]{2,1,0:T(8,128)(2,1)S(1)}, bf16[256,32,256]{2,1,0:T(8,128)(2,1)}, u32[]{:S(2)}) %copy-start) | copy-done | bytes 4194328
  134.4 0.0 copy-start.1
  134.4 0.7 copy-done.1
  135.1 3.6 %shard_map.47 = f32[32,16384]{1,0:T(8,128)} custom-call(s32[256]{0:T(256)S(1)} %copy-done.1, bf16[256,32,256]{2,1,0:T(8,128)(2,1)S(1)} %copy-done), custom_call_target="tpu_custom_call" | custom-call | tf_op jit(solution)/shard_map/pallas_call | solution.py:287
Async XLA Ops:
  132.2 2.2 %copy-start = (bf16[256,32,256]{2,1,0:T(8,128)(2,1)S(1)}, bf16[256,32,256]{2,1,0:T(8,128)(2,1)}, u32[]{:S(2)}) copy-start(bf16[256,32,256]{2,1,0:T(8,128)(2,1)} %get-tuple-element.8.back_ref) | copy-start | bytes 12582916
  134.4 0.7 copy-start.1

commit v3 on v2

v3 whole, which is shorter than its diff:
```python
import functools
import math

import jax
import jax.numpy as jnp
from jax import lax
from jax.experimental import pallas as pl
from jax.experimental.pallas import tpu as pltpu
from jax.sharding import PartitionSpec as P

P_SIZE = 256
HALF = 16
X_STEPS = 32767.0 / 2.4
A_STEPS = 32767.0 / 2.0
FOUR_PI = 4.0 * math.pi
MESH = pl.DeviceIdType.MESH


def thirds(value):
    high = value.astype(jnp.bfloat16).astype(jnp.float32)
    rest = value - high
    mid = rest.astype(jnp.bfloat16).astype(jnp.float32)
    return high, mid, rest - mid


def column(row):
    count = row.shape[1]
    down = lax.broadcasted_iota(jnp.int32, (count, count), 0)
    across = lax.broadcasted_iota(jnp.int32, (count, count), 1)
    return jnp.sum(jnp.where(down == across, row, 0), axis=1, keepdims=True)


def slot_table(pair_ids, kinds, local_count):
    slots = pair_ids.shape[1]
    ends = 2 * slots
    left, right = pair_ids[0:1], pair_ids[1:2]
    ids = jnp.concatenate([left, right], axis=1)
    holder = lax.div(ids, local_count)
    down = lax.broadcasted_iota(jnp.int32, (ends, ends), 0)
    across = lax.broadcasted_iota(jnp.int32, (ends, ends), 1)
    holder_down = column(holder)
    same = holder_down == holder
    rank = jnp.sum(jnp.where(same & (down < across), 1, 0), axis=0, keepdims=True)
    rank_down = jnp.sum(jnp.where(same & (across < down), 1, 0), axis=1, keepdims=True)
    place = 2 * holder + rank
    other = jnp.concatenate([place[:, slots:], place[:, :slots]], axis=1)
    live = jnp.where(kinds > 0, 1, 0)
    twice = jnp.where(left != right, live, 0)
    keep = jnp.concatenate([live, twice], axis=1)
    admissible = jnp.where(kinds == 2, 1, 0)
    admissible = jnp.concatenate([admissible, admissible], axis=1)
    code = lax.rem(ids, local_count) + 64 * other + 16384 * admissible + 32768 * keep
    code_down = column(code)
    place_down = 2 * holder_down + rank_down
    table = jnp.sum(jnp.where(place_down == across, code_down, 0), axis=0, keepdims=True)
    asked = (code_down & 63) * (1 + 63 * rank_down)
    lanes = lax.broadcasted_iota(jnp.int32, (ends, 128), 1)
    request = jnp.sum(jnp.where(holder_down == lanes, asked, 0), axis=0, keepdims=True)
    return table, request


def exchange_kernel(
    groups, members, side,
    pair_ref, kind_ref, modes_ref, geo_ref,
    back_ref, wanted_ref,
    code_vmem, code_smem, row_vmem, asked_vmem, asked_smem,
    mode_blocks, geo_blocks, geo_stage, geo_got,
    mode_stage, first_got, second_got, mode_back, tiles,
    send_sems, recv_sems, local_sem,
):
    devices = groups * members
    others = devices - 1
    local_count = geo_blocks.shape[0]
    grp = lax.axis_index("grp")
    dev = lax.axis_index("dev")
    me = grp * members + dev
    member_bits = members.bit_length() - 1
    side_bits = side.bit_length() - 1

    def partner_of(step):
        shift = (step * 45) & (devices - 1)
        dg, dv = shift >> member_bits, shift & (members - 1)
        y = ((grp >> 1) + (dg >> 1)) & (groups // 2 - 1)
        core = (grp + dg) & 1
        x = ((dev >> side_bits) + (dv >> side_bits)) & (side - 1)
        z = (dev + dv) & (side - 1)
        return y * 2 + core, x * side + z

    def in_row(shift):
        return grp, (dev + shift) & (members - 1)

    def in_column(shift):
        return (grp + shift) & (groups - 1), dev

    def two_steps(passes, body):
        @pl.loop(0, passes)
        def _(index):
            for step in (2 * index + 1, 2 * index + 2):
                place = partner_of(step)
                body(step, place, place[0] * members + place[1])

    def send(source, target, which, place):
        pltpu.make_async_remote_copy(
            src_ref=source, dst_ref=target,
            send_sem=send_sems.at[which], recv_sem=recv_sems.at[which],
            device_id=place, device_id_type=MESH,
        ).start()

    def drain(source, target, which):
        return pltpu.make_async_remote_copy(
            src_ref=source, dst_ref=target,
            send_sem=send_sems.at[which], recv_sem=recv_sems.at[which],
            device_id=(grp, dev), device_id_type=MESH,
        )

    barrier = pltpu.get_barrier_semaphore()
    for shift in range(1, members):
        pl.semaphore_signal(barrier, inc=1, device_id=in_row(shift), device_id_type=MESH)
    for shift in range(1, groups):
        pl.semaphore_signal(barrier, inc=1, device_id=in_column(shift), device_id_type=MESH)

    table, request = slot_table(pair_ref[...], kind_ref[...], local_count)
    row_vmem[...] = request
    asked_vmem[me] = request
    code_vmem[...] = table
    local = pltpu.make_async_copy(code_vmem, code_smem, local_sem)
    local.start()
    high_rows = lax.broadcasted_iota(jnp.int32, (4, P_SIZE), 0)
    steps = jnp.where(high_rows < 3, X_STEPS, A_STEPS)
    for cluster in range(local_count):
        panels = slice(cluster * P_SIZE, (cluster + 1) * P_SIZE)
        mode_blocks[0, cluster] = modes_ref[0:HALF, panels]
        mode_blocks[1, cluster] = modes_ref[HALF : 2 * HALF, panels]
        geo_blocks[cluster] = jnp.round(geo_ref[:, panels] * steps)
    local.wait()
    pl.semaphore_wait(barrier, members + groups - 2)

    for shift in range(1, members):
        send(row_vmem, asked_vmem.at[me], 0, in_row(shift))
    along_row = drain(asked_vmem.at[pl.ds(0, members - 1)], asked_vmem.at[pl.ds(0, members - 1)], 0)
    along_row.wait_recv()
    for shift in range(1, groups):
        mine = asked_vmem.at[pl.ds(grp * members, members)]
        send(mine, mine, 1, in_column(shift))
    far = asked_vmem.at[pl.ds(0, members * (groups - 1))]
    along_column = drain(far, far, 1)
    along_column.wait_recv()
    local = pltpu.make_async_copy(asked_vmem, asked_smem, local_sem)
    local.start()
    local.wait()

    def wanted(to, rank):
        return (asked_smem[to, 0, me] >> (6 * rank)) & 63

    def geo_for(to):
        both = jnp.concatenate([geo_blocks[wanted(to, 0)], geo_blocks[wanted(to, 1)]], axis=0)
        both = jnp.concatenate([both[:, :128], both[:, 128:]], axis=0)
        return both.astype(jnp.int32).astype(jnp.int16)

    def send_geo(step, place, to):
        geo_stage[to] = geo_for(to)
        send(geo_stage.at[to], geo_got.at[me], 2, place)

    def send_modes(half, got):
        def body(step, place, to):
            for rank in range(2):
                mode_stage[half, 2 * to + rank] = mode_blocks[half, wanted(to, rank)]
            send(
                mode_stage.at[half, pl.ds(2 * to, 2)], got.at[pl.ds(2 * me, 2)], 3 + half, place
            )
        return body

    def all_partners(body):
        two_steps(others // 2, body)
        place = partner_of(others)
        body(others, place, place[0] * members + place[1])

    all_partners(send_geo)
    all_partners(send_modes(0, first_got))
    all_partners(send_modes(1, second_got))
    geo_got[me] = geo_for(me)
    for rank in range(2):
        first_got[2 * me + rank] = mode_blocks[0, wanted(me, rank)]
        second_got[2 * me + rank] = mode_blocks[1, wanted(me, rank)]

    @pl.loop(0, devices)
    def _(to):
        for rank in range(2):
            wanted_ref[2 * to + rank] = wanted(to, rank)

    geos = drain(geo_stage.at[pl.ds(0, others)], geo_got.at[pl.ds(0, others)], 2)
    geos.wait_recv()

    row = lax.broadcasted_iota(jnp.int32, (8, P_SIZE), 0)
    scale = jnp.where(
        (row & 3) < 3, FOUR_PI / X_STEPS, FOUR_PI * FOUR_PI / A_STEPS
    )

    def both_clusters(source):
        block = geo_got[source].astype(jnp.int32).astype(jnp.float32)
        return jnp.concatenate([block[0:8], block[8:16]], axis=1) * scale

    def length(block, factor):
        square = block * block
        return square[0:1] + square[1:2] + square[2:3] + block[3:4] * factor

    def tile_of(to, rank):
        code = code_smem[0, 2 * to + rank]
        other = (code >> 6) & 255
        factor = jnp.where((code & 16384) != 0, jnp.float32(0.1), jnp.float32(1.0))
        mine = both_clusters(to)
        theirs = both_clusters(other >> 1)
        if rank == 1:
            mine = pltpu.roll(mine, 4, 0)
        theirs = jnp.where((other & 1) == 1, pltpu.roll(theirs, 4, 0), theirs)
        norm = length(mine, factor)
        right = jnp.where(row < 3, mine, jnp.where(row == 3, norm, jnp.where(row == 4, 1.0, 0.0)))
        norm = length(theirs, factor)
        left = jnp.where(
            row < 3, -2.0 * theirs, jnp.where(row == 3, 1.0, jnp.where(row == 4, norm, 0.0))
        )
        a, b, c = thirds(left)
        left = jnp.concatenate([a, b, a, b, c, a], axis=0).astype(jnp.bfloat16)
        a, b, c = thirds(right)
        right = jnp.concatenate([a, a, b, b, a, c], axis=0).astype(jnp.bfloat16)
        squared = lax.dot_general(
            left, right, (((0,), (0,)), ((), ())), preferred_element_type=jnp.float32
        )
        return lax.rsqrt(squared).astype(jnp.bfloat16)

    def make_tiles(step, place, to):
        for rank in range(2):
            tiles[2 * (step - 1) + rank] = tile_of(to, rank)

    two_steps(devices // 2, make_tiles)

    def product(half, got, step, to, rank):
        code = code_smem[0, 2 * to + rank]
        keep = ((code >> 15) & 1).astype(jnp.float32)
        out = jnp.dot(
            got[(code >> 6) & 255], tiles[2 * (step - 1) + rank], preferred_element_type=jnp.float32
        )
        mode_back[half, 2 * to + rank] = (out * keep).astype(jnp.bfloat16)

    def return_half(half, got):
        def give_back(to, place):
            send(
                mode_back.at[half, pl.ds(2 * to, 2)], back_ref.at[half, pl.ds(2 * me, 2)],
                5 + half, place,
            )

        def two_products(first, second):
            places = []
            for step in (first, second):
                place = partner_of(step)
                to = place[0] * members + place[1]
                places.append((to, place))
                for rank in range(2):
                    product(half, got, step, to, rank)
            return places

        @pl.loop(0, devices // 2 - 1)
        def _(index):
            for to, place in two_products(2 * index + 1, 2 * index + 2):
                give_back(to, place)

        give_back(*two_products(others, devices)[0])

    gots = []
    for half, got in enumerate((first_got, second_got)):
        arrived = drain(
            mode_stage.at[half, pl.ds(0, 2 * others)], got.at[pl.ds(0, 2 * others)], 3 + half
        )
        arrived.wait_recv()
        gots.append(arrived)
        return_half(half, got)

    for half in range(2):
        own = pltpu.make_async_copy(
            mode_back.at[half, pl.ds(2 * me, 2)], back_ref.at[half, pl.ds(2 * me, 2)], local_sem
        )
        own.start()
        own.wait()
    for half in range(2):
        backs = drain(
            mode_back.at[half, pl.ds(0, 2 * others)], back_ref.at[half, pl.ds(0, 2 * others)],
            5 + half,
        )
        backs.wait_recv()
        backs.wait_send()
    along_row.wait_send()
    along_column.wait_send()
    geos.wait_send()
    for arrived in gots:
        arrived.wait_send()


def sum_kernel(chunks, wanted_ref, back_ref, out_ref, arrived, total, in_sems, out_sems):
    ends = back_ref.shape[1]
    count = ends // chunks

    def piece(half, chunk):
        part = pl.ds(chunk * count, count)
        return pltpu.make_async_copy(
            back_ref.at[half, part], arrived.at[half, part], in_sems.at[half * chunks + chunk]
        )

    for half in range(2):
        for chunk in range(chunks):
            piece(half, chunk).start()
    total[...] = jnp.zeros_like(total)
    written = []
    for half in range(2):
        rows = pl.ds(half * HALF, HALF)
        for chunk in range(chunks):
            piece(half, chunk).wait()

            @pl.loop(0, count, unroll=8)
            def _(index):
                slot = chunk * count + index
                place = pl.ds(pl.multiple_of(wanted_ref[slot] * P_SIZE, P_SIZE), P_SIZE)
                total[rows, place] += arrived[half, slot].astype(jnp.float32)

        written.append(pltpu.make_async_copy(total.at[rows], out_ref.at[rows], out_sems.at[half]))
        written[-1].start()
    for copy in written:
        copy.wait()


def local(modes, geometry, pair_list, pair_kind):
    groups = lax.axis_size("grp")
    members = lax.axis_size("dev")
    devices = groups * members
    side = math.isqrt(members)
    local_count = modes.shape[1] // P_SIZE
    slots = pair_list.shape[0]
    ends = 2 * slots

    vmem = pl.BlockSpec(memory_space=pltpu.VMEM)
    smem = pl.BlockSpec(memory_space=pltpu.SMEM)
    back, wanted = pl.pallas_call(
        functools.partial(exchange_kernel, groups, members, side),
        out_shape=[
            jax.ShapeDtypeStruct((2, ends, HALF, P_SIZE), jnp.bfloat16),
            jax.ShapeDtypeStruct((ends,), jnp.int32),
        ],
        in_specs=[vmem, vmem, vmem, vmem],
        out_specs=[pl.BlockSpec(memory_space=pl.ANY), smem],
        scratch_shapes=[
            pltpu.VMEM((1, ends), jnp.int32),
            pltpu.SMEM((1, ends), jnp.int32),
            pltpu.VMEM((1, 128), jnp.int32),
            pltpu.VMEM((devices, 1, 128), jnp.int32),
            pltpu.SMEM((devices, 1, 128), jnp.int32),
            pltpu.VMEM((2, local_count, HALF, P_SIZE), jnp.bfloat16),
            pltpu.VMEM((local_count, 4, P_SIZE), jnp.float32),
            pltpu.VMEM((devices, 16, 128), jnp.int16),
            pltpu.VMEM((devices, 16, 128), jnp.int16),
            pltpu.VMEM((2, ends, HALF, P_SIZE), jnp.bfloat16),
            pltpu.VMEM((ends, HALF, P_SIZE), jnp.bfloat16),
            pltpu.VMEM((ends, HALF, P_SIZE), jnp.bfloat16),
            pltpu.VMEM((2, ends, HALF, P_SIZE), jnp.bfloat16),
            pltpu.VMEM((ends, P_SIZE, P_SIZE), jnp.bfloat16),
            pltpu.SemaphoreType.DMA((7,)),
            pltpu.SemaphoreType.DMA((7,)),
            pltpu.SemaphoreType.DMA,
        ],
        compiler_params=pltpu.CompilerParams(
            collective_id=0, has_side_effects=True, vmem_limit_bytes=56 * 1024 * 1024
        ),
    )(pair_list.T, pair_kind.reshape(1, slots), modes, geometry)

    chunks = 4
    anywhere = pl.BlockSpec(memory_space=pl.ANY)
    return pl.pallas_call(
        functools.partial(sum_kernel, chunks),
        out_shape=jax.ShapeDtypeStruct((2 * HALF, local_count * P_SIZE), jnp.float32),
        in_specs=[smem, anywhere],
        out_specs=anywhere,
        scratch_shapes=[
            pltpu.VMEM((2, ends, HALF, P_SIZE), jnp.bfloat16),
            pltpu.VMEM((2 * HALF, local_count * P_SIZE), jnp.float32),
            pltpu.SemaphoreType.DMA((2 * chunks,)),
            pltpu.SemaphoreType.DMA((2,)),
        ],
        compiler_params=pltpu.CompilerParams(vmem_limit_bytes=56 * 1024 * 1024),
    )(wanted, back)


def solution(mesh):
    placed = (
        P(None, ("grp", "dev")),
        P(None, ("grp", "dev")),
        P(("grp", "dev"), None),
        P(("grp", "dev")),
    )
    return jax.shard_map(
        local, mesh=mesh, in_specs=placed, out_specs=P(None, ("grp", "dev")), check_vma=False
    )
```

time: 139 us -> 125 us (0.90)
  Pallas kernels: 136 us -> 125 us
  local copies, waits for them, and re-layouts: 2.86 us -> 0 us
    pallas_call x2, Pallas kernels: 136 us -> 125 us  [the longest x1 120 us: local(): pl.pallas_call(functools.partial(exchange_kernel, groups, members, side),...]
    unnamed x4 -> x0, local copies, waits for them, and re-layouts: 2.86 us -> none
where the time goes in v3:
time: 125 us
  Pallas kernels  125 us (100%)
    pallas_call x1, Pallas kernels, local(): pl.pallas_call(functools.partial(exchange_kernel, groups, members, side),...  120 us
    pallas_call x1, Pallas kernels, local(): pl.pallas_call(functools.partial(sum_kernel, chunks), out_shape=jax.Shape...  4.93 us

profile of v3, /device:TPU:1, one launch (start us, length us, event | category | flops | bytes accessed | tf_op | source)
XLA Modules:
  0.0 125.0 jit_solution(16347262130906380861)
XLA Ops:
  0.0 120.1 %shard_map.46 = (bf16[2,256,16,256]{3,2,1,0:T(8,128)(2,1)}, s32[256]{0:T(256)}) custom-call(s32[2,128]{1,0:T(2,128)} %bitcast.2, s32[1,128]{1,0:T(1,128)} %bitcast.3, bf16[32,16384]{1,0:T(8,128)(2,1)} %modes_ref.1, f32[4,16384]{1,0:T(4,128)} %geo_ref.1), custom_call_target="tpu_custom_call" | custom-call | tf_op jit(solution)/shard_map/pallas_call | solution.py:341
  120.1 4.9 %shard_map.47 = f32[32,16384]{1,0:T(8,128)} custom-call(s32[256]{0:T(256)} %get-tuple-element.7.wanted_ref, bf16[2,256,16,256]{3,2,1,0:T(8,128)(2,1)} %get-tuple-element.8.back_ref), custom_call_target="tpu_custom_call" | custom-call | tf_op jit(solution)/shard_map/pallas_call | solution.py:375

commit v4 on v3

--- a/solution.py
+++ b/solution.py
@@ -61,12 +61,13 @@
 
 def exchange_kernel(
     groups, members, side,
+    pair_hbm, kind_hbm, modes_hbm, geo_hbm,
+    back_ref, wanted_ref,
     pair_ref, kind_ref, modes_ref, geo_ref,
-    back_ref, wanted_ref,
     code_vmem, code_smem, row_vmem, asked_vmem, asked_smem,
     mode_blocks, geo_blocks, geo_stage, geo_got,
     mode_stage, first_got, second_got, mode_back, tiles,
-    send_sems, recv_sems, local_sem,
+    send_sems, recv_sems, cell_sems, row_sems, local_sem, input_sems,
 ):
     devices = groups * members
     others = devices - 1
@@ -78,7 +79,7 @@
     side_bits = side.bit_length() - 1
 
     def partner_of(step):
-        shift = (step * 45) & (devices - 1)
+        shift = (step * 11) & (devices - 1)
         dg, dv = shift >> member_bits, shift & (members - 1)
         y = ((grp >> 1) + (dg >> 1)) & (groups // 2 - 1)
         core = (grp + dg) & 1
@@ -86,11 +87,31 @@
         z = (dev + dv) & (side - 1)
         return y * 2 + core, x * side + z
 
-    def in_row(shift):
-        return grp, (dev + shift) & (members - 1)
-
-    def in_column(shift):
-        return (grp + shift) & (groups - 1), dev
+    cell = devices // 8
+    fold = side // 2
+    fold_bits = fold.bit_length() - 1
+    my_y, my_core, my_x, my_z = grp >> 1, grp & 1, dev >> side_bits, dev & (side - 1)
+
+    def key_of(place):
+        y, core, x, z = place[0] >> 1, place[0] & 1, place[1] >> side_bits, place[1] & (side - 1)
+        which = (y & 1) * 4 + (x & 1) * 2 + (z & 1)
+        return which * cell + (((y >> 1) * fold + (x >> 1)) * fold + (z >> 1)) * 2 + core
+
+    def at(dy, core, dx, dz):
+        y = (my_y + dy) & (groups // 2 - 1)
+        x, z = (my_x + dx) & (side - 1), (my_z + dz) & (side - 1)
+        return y * 2 + ((my_core + core) & 1), x * side + z
+
+    def in_cell(which, index):
+        z = (index >> 1) & (fold - 1)
+        x = (index >> (1 + fold_bits)) & (fold - 1)
+        y = index >> (1 + 2 * fold_bits)
+        return at(
+            ((which >> 2) & 1) + 2 * y, index & 1, ((which >> 1) & 1) + 2 * x, (which & 1) + 2 * z
+        )
+
+    my_key = key_of((grp, dev))
+    my_rows = pl.ds(my_key // cell * cell, cell)
 
     def two_steps(passes, body):
         @pl.loop(0, passes)
@@ -114,43 +135,65 @@
         )
 
     barrier = pltpu.get_barrier_semaphore()
-    for shift in range(1, members):
-        pl.semaphore_signal(barrier, inc=1, device_id=in_row(shift), device_id_type=MESH)
-    for shift in range(1, groups):
-        pl.semaphore_signal(barrier, inc=1, device_id=in_column(shift), device_id_type=MESH)
-
+    for index in range(1, cell):
+        pl.semaphore_signal(barrier, inc=1, device_id=in_cell(0, index), device_id_type=MESH)
+    for which in range(1, 8):
+        source = at(-(which >> 2), 0, -((which >> 1) & 1), -(which & 1))
+        pl.semaphore_signal(barrier, inc=1, device_id=source, device_id_type=MESH)
+
+    inputs = [
+        pltpu.make_async_copy(source, target, input_sems.at[index])
+        for index, (source, target) in enumerate((
+            (pair_hbm, pair_ref), (kind_hbm, kind_ref), (geo_hbm, geo_ref), (modes_hbm, modes_ref),
+        ))
+    ]
+    for copy in inputs:
+        copy.start()
+    inputs[0].wait()
+    inputs[1].wait()
     table, request = slot_table(pair_ref[...], kind_ref[...], local_count)
     row_vmem[...] = request
-    asked_vmem[me] = request
+    asked_vmem[my_key] = request
     code_vmem[...] = table
     local = pltpu.make_async_copy(code_vmem, code_smem, local_sem)
     local.start()
     high_rows = lax.broadcasted_iota(jnp.int32, (4, P_SIZE), 0)
     steps = jnp.where(high_rows < 3, X_STEPS, A_STEPS)
+    inputs[2].wait()
+    inputs[3].wait()
     for cluster in range(local_count):
         panels = slice(cluster * P_SIZE, (cluster + 1) * P_SIZE)
         mode_blocks[0, cluster] = modes_ref[0:HALF, panels]
         mode_blocks[1, cluster] = modes_ref[HALF : 2 * HALF, panels]
         geo_blocks[cluster] = jnp.round(geo_ref[:, panels] * steps)
     local.wait()
-    pl.semaphore_wait(barrier, members + groups - 2)
-
-    for shift in range(1, members):
-        send(row_vmem, asked_vmem.at[me], 0, in_row(shift))
-    along_row = drain(asked_vmem.at[pl.ds(0, members - 1)], asked_vmem.at[pl.ds(0, members - 1)], 0)
-    along_row.wait_recv()
-    for shift in range(1, groups):
-        mine = asked_vmem.at[pl.ds(grp * members, members)]
-        send(mine, mine, 1, in_column(shift))
-    far = asked_vmem.at[pl.ds(0, members * (groups - 1))]
-    along_column = drain(far, far, 1)
-    along_column.wait_recv()
-    local = pltpu.make_async_copy(asked_vmem, asked_smem, local_sem)
+    pl.semaphore_wait(barrier, cell + 6)
+
+    for index in range(1, cell):
+        send(row_vmem, asked_vmem.at[my_key], 0, in_cell(0, index))
+    in_own = drain(asked_vmem.at[pl.ds(0, cell - 1)], asked_vmem.at[pl.ds(0, cell - 1)], 0)
+    in_own.wait_recv()
+
+    def across(which):
+        return pltpu.make_async_remote_copy(
+            src_ref=asked_vmem.at[my_rows], dst_ref=asked_vmem.at[my_rows],
+            send_sem=send_sems.at[1], recv_sem=cell_sems.at[which],
+            device_id=in_cell(which, 0), device_id_type=MESH,
+        )
+
+    def readable(which):
+        rows = pl.ds(key_of(in_cell(which, 0)) // cell * cell, cell)
+        return pltpu.make_async_copy(asked_vmem.at[rows], asked_smem.at[rows], row_sems.at[which])
+
+    for which in range(1, 8):
+        across(which).start()
+    local = readable(0)
     local.start()
     local.wait()
 
     def wanted(to, rank):
-        return (asked_smem[to, 0, me] >> (6 * rank)) & 63
+        place = (to >> member_bits, to & (members - 1))
+        return (asked_smem[key_of(place), 0, me] >> (6 * rank)) & 63
 
     def geo_for(to):
         both = jnp.concatenate([geo_blocks[wanted(to, 0)], geo_blocks[wanted(to, 1)]], axis=0)
@@ -170,14 +213,44 @@
             )
         return body
 
-    def all_partners(body):
-        two_steps(others // 2, body)
-        place = partner_of(others)
-        body(others, place, place[0] * members + place[1])
-
-    all_partners(send_geo)
-    all_partners(send_modes(0, first_got))
-    all_partners(send_modes(1, second_got))
+    def at_place(place, body):
+        body(0, place, place[0] * members + place[1])
+
+    send_first = send_modes(0, first_got)
+    send_second = send_modes(1, second_got)
+
+    for body in (send_geo, send_first, send_second):
+        @pl.loop(1, cell)
+        def _(index):
+            at_place(in_cell(0, index), body)
+
+    def geos_for(which):
+        readable(which).wait()
+
+        @pl.loop(0, cell // 2)
+        def _(index):
+            at_place(in_cell(which, 2 * index), send_geo)
+            at_place(in_cell(which, 2 * index + 1), send_geo)
+
+    across(1).wait_recv()
+    readable(1).start()
+
+    @pl.loop(1, 7)
+    def _(which):
+        across(which + 1).wait_recv()
+        readable(which + 1).start()
+        geos_for(which)
+
+    geos_for(7)
+
+    away = 7 * cell
+    for body in (send_first, send_second):
+        @pl.loop(0, away // 2)
+        def _(index):
+            for step in (2 * index, 2 * index + 1):
+                turn = lax.rem(step * 11, away)
+                at_place(in_cell(1 + (turn >> (cell.bit_length() - 1)), turn & (cell - 1)), body)
+
     geo_got[me] = geo_for(me)
     for rank in range(2):
         first_got[2 * me + rank] = mode_blocks[0, wanted(me, rank)]
@@ -288,14 +361,15 @@
         )
         backs.wait_recv()
         backs.wait_send()
-    along_row.wait_send()
-    along_column.wait_send()
+    in_own.wait_send()
+    others_rows = asked_vmem.at[pl.ds(0, away)]
+    drain(others_rows, others_rows, 1).wait_send()
     geos.wait_send()
     for arrived in gots:
         arrived.wait_send()
 
 
-def sum_kernel(chunks, wanted_ref, back_ref, out_ref, arrived, total, in_sems, out_sems):
+def sum_kernel(chunks, wanted_ref, back_ref, out_ref, arrived, first, second, in_sems, out_sems):
     ends = back_ref.shape[1]
     count = ends // chunks
 
@@ -305,23 +379,29 @@
             back_ref.at[half, part], arrived.at[half, part], in_sems.at[half * chunks + chunk]
         )
 
-    for half in range(2):
-        for chunk in range(chunks):
+    for chunk in range(chunks):
+        for half in range(2):
             piece(half, chunk).start()
-    total[...] = jnp.zeros_like(total)
+    first[...] = jnp.zeros_like(first)
+    second[...] = jnp.zeros_like(second)
+    for chunk in range(chunks):
+        for half in range(2):
+            piece(half, chunk).wait()
+
+        @pl.loop(0, count, unroll=8)
+        def _(index):
+            slot = chunk * count + index
+            place = pl.ds(pl.multiple_of(wanted_ref[slot] * P_SIZE, P_SIZE), P_SIZE)
+            one = arrived[0, slot].astype(jnp.float32)
+            two = arrived[1, slot].astype(jnp.float32)
+            one_total, two_total = first[:, place], second[:, place]
+            first[:, place] = one_total + one
+            second[:, place] = two_total + two
+
     written = []
-    for half in range(2):
+    for half, total in enumerate((first, second)):
         rows = pl.ds(half * HALF, HALF)
-        for chunk in range(chunks):
-            piece(half, chunk).wait()
-
-            @pl.loop(0, count, unroll=8)
-            def _(index):
-                slot = chunk * count + index
-                place = pl.ds(pl.multiple_of(wanted_ref[slot] * P_SIZE, P_SIZE), P_SIZE)
-                total[rows, place] += arrived[half, slot].astype(jnp.float32)
-
-        written.append(pltpu.make_async_copy(total.at[rows], out_ref.at[rows], out_sems.at[half]))
+        written.append(pltpu.make_async_copy(total, out_ref.at[rows], out_sems.at[half]))
         written[-1].start()
     for copy in written:
         copy.wait()
@@ -336,7 +416,7 @@
     slots = pair_list.shape[0]
     ends = 2 * slots
 
-    vmem = pl.BlockSpec(memory_space=pltpu.VMEM)
+    anywhere = pl.BlockSpec(memory_space=pl.ANY)
     smem = pl.BlockSpec(memory_space=pltpu.SMEM)
     back, wanted = pl.pallas_call(
         functools.partial(exchange_kernel, groups, members, side),
@@ -344,9 +424,13 @@
             jax.ShapeDtypeStruct((2, ends, HALF, P_SIZE), jnp.bfloat16),
             jax.ShapeDtypeStruct((ends,), jnp.int32),
         ],
-        in_specs=[vmem, vmem, vmem, vmem],
+        in_specs=[anywhere, anywhere, anywhere, anywhere],
         out_specs=[pl.BlockSpec(memory_space=pl.ANY), smem],
         scratch_shapes=[
+            pltpu.VMEM((2, slots), jnp.int32),
+            pltpu.VMEM((1, slots), jnp.int32),
+            pltpu.VMEM(modes.shape, modes.dtype),
+            pltpu.VMEM(geometry.shape, geometry.dtype),
             pltpu.VMEM((1, ends), jnp.int32),
             pltpu.SMEM((1, ends), jnp.int32),
             pltpu.VMEM((1, 128), jnp.int32),
@@ -363,15 +447,17 @@
             pltpu.VMEM((ends, P_SIZE, P_SIZE), jnp.bfloat16),
             pltpu.SemaphoreType.DMA((7,)),
             pltpu.SemaphoreType.DMA((7,)),
+            pltpu.SemaphoreType.DMA((8,)),
+            pltpu.SemaphoreType.DMA((8,)),
             pltpu.SemaphoreType.DMA,
+            pltpu.SemaphoreType.DMA((4,)),
         ],
         compiler_params=pltpu.CompilerParams(
             collective_id=0, has_side_effects=True, vmem_limit_bytes=56 * 1024 * 1024
         ),
     )(pair_list.T, pair_kind.reshape(1, slots), modes, geometry)
 
-    chunks = 4
-    anywhere = pl.BlockSpec(memory_space=pl.ANY)
+    chunks = min(8, ends // 8)
     return pl.pallas_call(
         functools.partial(sum_kernel, chunks),
         out_shape=jax.ShapeDtypeStruct((2 * HALF, local_count * P_SIZE), jnp.float32),
@@ -379,7 +465,8 @@
         out_specs=anywhere,
         scratch_shapes=[
             pltpu.VMEM((2, ends, HALF, P_SIZE), jnp.bfloat16),
-            pltpu.VMEM((2 * HALF, local_count * P_SIZE), jnp.float32),
+            pltpu.VMEM((HALF, local_count * P_SIZE), jnp.float32),
+            pltpu.VMEM((HALF, local_count * P_SIZE), jnp.float32),
             pltpu.SemaphoreType.DMA((2 * chunks,)),
             pltpu.SemaphoreType.DMA((2,)),
         ],

time: 125 us -> 122 us (0.976)
  Pallas kernels: 125 us -> 121 us
    pallas_call x1, Pallas kernels: 120 us -> 117 us  [local(): pl.pallas_call(functools.partial(exchange_kernel, groups, members, side),...]
where the time goes in v4:
time: 122 us; the launch traced here: 121 us
  Pallas kernels  121 us (99%)
    pallas_call x1, Pallas kernels, local(): pl.pallas_call(functools.partial(exchange_kernel, groups, members, side),...  117 us
    pallas_call x1, Pallas kernels, local(): pl.pallas_call(functools.partial(sum_kernel, chunks), out_shape=jax.Shape...  4.54 us

profile of v4, /device:TPU:1, one launch (start us, length us, event | category | flops | bytes accessed | tf_op | source)
XLA Modules:
  0.0 121.4 jit_solution(10007445708128273518)
XLA Ops:
  0.0 116.8 %shard_map.46 = (bf16[2,256,16,256]{3,2,1,0:T(8,128)(2,1)}, s32[256]{0:T(256)}) custom-call(s32[2,128]{1,0:T(2,128)} %bitcast.2, s32[1,128]{1,0:T(1,128)} %bitcast.3, bf16[32,16384]{1,0:T(8,128)(2,1)} %modes_hbm.1, f32[4,16384]{1,0:T(4,128)} %geo_hbm.1), custom_call_target="tpu_custom_call" | custom-call | tf_op jit(solution)/shard_map/pallas_call | solution.py:421
  116.9 4.5 %shard_map.47 = f32[32,16384]{1,0:T(8,128)} custom-call(s32[256]{0:T(256)} %get-tuple-element.7.wanted_ref, bf16[2,256,16,256]{3,2,1,0:T(8,128)(2,1)} %get-tuple-element.8.back_ref), custom_call_target="tpu_custom_call" | custom-call | tf_op jit(solution)/shard_map/pallas_call | solution.py:461

commit v5 on v4

--- a/solution.py
+++ b/solution.py
@@ -59,15 +59,34 @@
     return table, request
 
 
+def sum_table(ids, local_count):
+    ends = ids.shape[1]
+    down = lax.broadcasted_iota(jnp.int32, (ends, ends), 0)
+    across = lax.broadcasted_iota(jnp.int32, (ends, ends), 1)
+    ids_down = column(ids)
+    earlier = jnp.where((ids == ids_down) & (across < down), 1, 0)
+    earlier = jnp.sum(earlier, axis=1, keepdims=True)
+    place = earlier + jnp.sum(jnp.where(ids < ids_down, 1, 0), axis=1, keepdims=True)
+    slot = lax.broadcasted_iota(jnp.int32, (ends, 1), 0) + 256 * jnp.minimum(earlier, 1)
+    order = jnp.sum(jnp.where(place == across, slot, 0), axis=0, keepdims=True)
+    lanes = lax.broadcasted_iota(jnp.int32, (ends, 128), 1)
+    upto = jnp.sum(jnp.where(ids_down <= lanes, 1, 0), axis=0, keepdims=True)
+    here = jnp.sum(jnp.where(ids_down == lanes, 1, 0), axis=0, keepdims=True)
+    last = jnp.maximum(upto - 1, 0) + 256 * jnp.minimum(here, 1)
+    return order, last
+
+
 def exchange_kernel(
     groups, members, side,
     pair_hbm, kind_hbm, modes_hbm, geo_hbm,
-    back_ref, wanted_ref,
+    back_ref, total_ref, wanted_ref,
     pair_ref, kind_ref, modes_ref, geo_ref,
     code_vmem, code_smem, row_vmem, asked_vmem, asked_smem,
     mode_blocks, geo_blocks, geo_stage, geo_got,
     mode_stage, first_got, second_got, mode_back, tiles,
-    send_sems, recv_sems, cell_sems, row_sems, local_sem, input_sems,
+    wanted_smem, wanted_vmem, order_vmem, order_smem, last_vmem, last_smem,
+    first_back, staged, first_total,
+    send_sems, recv_sems, column_sems, row_sems, local_sem, input_sems,
 ):
     devices = groups * members
     others = devices - 1
@@ -79,7 +98,7 @@
     side_bits = side.bit_length() - 1
 
     def partner_of(step):
-        shift = (step * 11) & (devices - 1)
+        shift = (step * 107) & (devices - 1)
         dg, dv = shift >> member_bits, shift & (members - 1)
         y = ((grp >> 1) + (dg >> 1)) & (groups // 2 - 1)
         core = (grp + dg) & 1
@@ -87,38 +106,28 @@
         z = (dev + dv) & (side - 1)
         return y * 2 + core, x * side + z
 
-    cell = devices // 8
-    fold = side // 2
-    fold_bits = fold.bit_length() - 1
     my_y, my_core, my_x, my_z = grp >> 1, grp & 1, dev >> side_bits, dev & (side - 1)
-
-    def key_of(place):
-        y, core, x, z = place[0] >> 1, place[0] & 1, place[1] >> side_bits, place[1] & (side - 1)
-        which = (y & 1) * 4 + (x & 1) * 2 + (z & 1)
-        return which * cell + (((y >> 1) * fold + (x >> 1)) * fold + (z >> 1)) * 2 + core
 
     def at(dy, core, dx, dz):
         y = (my_y + dy) & (groups // 2 - 1)
         x, z = (my_x + dx) & (side - 1), (my_z + dz) & (side - 1)
         return y * 2 + ((my_core + core) & 1), x * side + z
 
-    def in_cell(which, index):
-        z = (index >> 1) & (fold - 1)
-        x = (index >> (1 + fold_bits)) & (fold - 1)
-        y = index >> (1 + 2 * fold_bits)
-        return at(
-            ((which >> 2) & 1) + 2 * y, index & 1, ((which >> 1) & 1) + 2 * x, (which & 1) + 2 * z
-        )
-
-    my_key = key_of((grp, dev))
-    my_rows = pl.ds(my_key // cell * cell, cell)
+    def in_column(which, index):
+        return at(index >> 1, index & 1, which >> side_bits, which & (side - 1))
+
+    my_key = dev * groups + grp
+    my_rows = pl.ds(dev * groups, groups)
+
+    def at_step(step, body):
+        place = partner_of(step)
+        body(step, place, place[0] * members + place[1])
 
     def two_steps(passes, body):
         @pl.loop(0, passes)
         def _(index):
             for step in (2 * index + 1, 2 * index + 2):
-                place = partner_of(step)
-                body(step, place, place[0] * members + place[1])
+                at_step(step, body)
 
     def send(source, target, which, place):
         pltpu.make_async_remote_copy(
@@ -135,11 +144,10 @@
         )
 
     barrier = pltpu.get_barrier_semaphore()
-    for index in range(1, cell):
-        pl.semaphore_signal(barrier, inc=1, device_id=in_cell(0, index), device_id_type=MESH)
-    for which in range(1, 8):
-        source = at(-(which >> 2), 0, -((which >> 1) & 1), -(which & 1))
-        pl.semaphore_signal(barrier, inc=1, device_id=source, device_id_type=MESH)
+    for which in range(1, members):
+        pl.semaphore_signal(barrier, inc=1, device_id=in_column(which, 0), device_id_type=MESH)
+    for index in range(1, groups):
+        pl.semaphore_signal(barrier, inc=1, device_id=in_column(0, index), device_id_type=MESH)
 
     inputs = [
         pltpu.make_async_copy(source, target, input_sems.at[index])
@@ -167,33 +175,34 @@
         mode_blocks[1, cluster] = modes_ref[HALF : 2 * HALF, panels]
         geo_blocks[cluster] = jnp.round(geo_ref[:, panels] * steps)
     local.wait()
-    pl.semaphore_wait(barrier, cell + 6)
-
-    for index in range(1, cell):
-        send(row_vmem, asked_vmem.at[my_key], 0, in_cell(0, index))
-    in_own = drain(asked_vmem.at[pl.ds(0, cell - 1)], asked_vmem.at[pl.ds(0, cell - 1)], 0)
+    pl.semaphore_wait(barrier, members + groups - 2)
+
+    for index in range(1, groups):
+        send(row_vmem, asked_vmem.at[my_key], 0, in_column(0, index))
+    in_own = drain(asked_vmem.at[pl.ds(0, groups - 1)], asked_vmem.at[pl.ds(0, groups - 1)], 0)
     in_own.wait_recv()
 
-    def across(which):
+    def across(which, mark):
         return pltpu.make_async_remote_copy(
             src_ref=asked_vmem.at[my_rows], dst_ref=asked_vmem.at[my_rows],
-            send_sem=send_sems.at[1], recv_sem=cell_sems.at[which],
-            device_id=in_cell(which, 0), device_id_type=MESH,
+            send_sem=send_sems.at[1], recv_sem=column_sems.at[mark],
+            device_id=in_column(which, 0), device_id_type=MESH,
         )
 
     def readable(which):
-        rows = pl.ds(key_of(in_cell(which, 0)) // cell * cell, cell)
+        rows = pl.ds(in_column(which, 0)[1] * groups, groups)
         return pltpu.make_async_copy(asked_vmem.at[rows], asked_smem.at[rows], row_sems.at[which])
 
-    for which in range(1, 8):
-        across(which).start()
+    for which in range(1, members):
+        back_x, back_z = -(which // side) % side, -which % side
+        across(which, back_x * side + back_z).start()
     local = readable(0)
     local.start()
     local.wait()
 
     def wanted(to, rank):
-        place = (to >> member_bits, to & (members - 1))
-        return (asked_smem[key_of(place), 0, me] >> (6 * rank)) & 63
+        key = (to & (members - 1)) * groups + (to >> member_bits)
+        return (asked_smem[key, 0, me] >> (6 * rank)) & 63
 
     def geo_for(to):
         both = jnp.concatenate([geo_blocks[wanted(to, 0)], geo_blocks[wanted(to, 1)]], axis=0)
@@ -219,37 +228,38 @@
     send_first = send_modes(0, first_got)
     send_second = send_modes(1, second_got)
 
-    for body in (send_geo, send_first, send_second):
-        @pl.loop(1, cell)
+    for body in (send_geo,):
+        @pl.loop(1, groups)
         def _(index):
-            at_place(in_cell(0, index), body)
+            at_place(in_column(0, index), body)
 
     def geos_for(which):
         readable(which).wait()
 
-        @pl.loop(0, cell // 2)
+        @pl.loop(0, groups // 2)
         def _(index):
-            at_place(in_cell(which, 2 * index), send_geo)
-            at_place(in_cell(which, 2 * index + 1), send_geo)
-
-    across(1).wait_recv()
+            at_place(in_column(which, 2 * index), send_geo)
+            at_place(in_column(which, 2 * index + 1), send_geo)
+
+    across(1, 1).wait_recv()
     readable(1).start()
 
-    @pl.loop(1, 7)
+    @pl.loop(1, members - 1)
     def _(which):
-        across(which + 1).wait_recv()
+        across(which + 1, which + 1).wait_recv()
         readable(which + 1).start()
         geos_for(which)
 
-    geos_for(7)
-
-    away = 7 * cell
+    geos_for(members - 1)
+
+    away = (members - 1) * groups
     for body in (send_first, send_second):
-        @pl.loop(0, away // 2)
+        @pl.loop(0, others // 2 + 1)
         def _(index):
-            for step in (2 * index, 2 * index + 1):
-                turn = lax.rem(step * 11, away)
-                at_place(in_cell(1 + (turn >> (cell.bit_length() - 1)), turn & (cell - 1)), body)
+            for step in (2 * index + 1, 2 * index + 2):
+                @pl.when(step != devices)
+                def _():
+                    at_step(step, body)
 
     geo_got[me] = geo_for(me)
     for rank in range(2):
@@ -259,7 +269,13 @@
     @pl.loop(0, devices)
     def _(to):
         for rank in range(2):
-            wanted_ref[2 * to + rank] = wanted(to, rank)
+            cluster = wanted(to, rank)
+            wanted_smem[0, 2 * to + rank] = cluster
+
+    def move(source, target):
+        copy = pltpu.make_async_copy(source, target, local_sem)
+        copy.start()
+        copy.wait()
 
     geos = drain(geo_stage.at[pl.ds(0, others)], geo_got.at[pl.ds(0, others)], 2)
     geos.wait_recv()
@@ -315,10 +331,12 @@
         )
         mode_back[half, 2 * to + rank] = (out * keep).astype(jnp.bfloat16)
 
+    backs = (first_back, back_ref)
+
     def return_half(half, got):
         def give_back(to, place):
             send(
-                mode_back.at[half, pl.ds(2 * to, 2)], back_ref.at[half, pl.ds(2 * me, 2)],
+                mode_back.at[half, pl.ds(2 * to, 2)], backs[half].at[pl.ds(2 * me, 2)],
                 5 + half, place,
             )
 
@@ -348,19 +366,37 @@
         gots.append(arrived)
         return_half(half, got)
 
-    for half in range(2):
-        own = pltpu.make_async_copy(
-            mode_back.at[half, pl.ds(2 * me, 2)], back_ref.at[half, pl.ds(2 * me, 2)], local_sem
-        )
-        own.start()
-        own.wait()
-    for half in range(2):
-        backs = drain(
-            mode_back.at[half, pl.ds(0, 2 * others)], back_ref.at[half, pl.ds(0, 2 * others)],
-            5 + half,
-        )
-        backs.wait_recv()
-        backs.wait_send()
+    for rank in range(2):
+        first_back[2 * me + rank] = mode_back[0, 2 * me + rank]
+    move(mode_back.at[1, pl.ds(2 * me, 2)], back_ref.at[pl.ds(2 * me, 2)])
+
+    move(wanted_smem, wanted_vmem)
+    move(wanted_vmem, wanted_ref)
+    order_vmem[...], last_vmem[...] = sum_table(wanted_vmem[...], local_count)
+    move(order_vmem, order_smem)
+    move(last_vmem, last_smem)
+    returned = [
+        drain(mode_back.at[half, pl.ds(0, 2 * others)], backs[half].at[pl.ds(0, 2 * others)], 5 + half)
+        for half in range(2)
+    ]
+    returned[0].wait_recv()
+
+    def add(index, total):
+        code = order_smem[0, index]
+        total = total * (code >> 8).astype(jnp.float32) + first_back[code & 255].astype(jnp.float32)
+        staged[index] = total
+        return total
+
+    lax.fori_loop(0, 2 * devices, add, jnp.zeros((HALF, P_SIZE), jnp.float32), unroll=4)
+    for cluster in range(local_count):
+        code = last_smem[0, cluster]
+        first_total[:, cluster * P_SIZE : (cluster + 1) * P_SIZE] = (
+            staged[code & 255] * (code >> 8).astype(jnp.float32)
+        )
+    move(first_total, total_ref)
+    returned[1].wait_recv()
+    for copy in returned:
+        copy.wait_send()
     in_own.wait_send()
     others_rows = asked_vmem.at[pl.ds(0, away)]
     drain(others_rows, others_rows, 1).wait_send()
@@ -369,40 +405,42 @@
         arrived.wait_send()
 
 
-def sum_kernel(chunks, wanted_ref, back_ref, out_ref, arrived, first, second, in_sems, out_sems):
-    ends = back_ref.shape[1]
+def sum_kernel(
+    chunks, wanted_hbm, back_ref, total_ref, out_ref, wanted_ref, arrived, first, second, in_sems, out_sems
+):
+    ends = back_ref.shape[0]
     count = ends // chunks
 
-    def piece(half, chunk):
+    def piece(chunk):
         part = pl.ds(chunk * count, count)
-        return pltpu.make_async_copy(
-            back_ref.at[half, part], arrived.at[half, part], in_sems.at[half * chunks + chunk]
-        )
-
+        return pltpu.make_async_copy(back_ref.at[part], arrived.at[part], in_sems.at[chunk])
+
+    known = pltpu.make_async_copy(wanted_hbm, wanted_ref, in_sems.at[chunks + 1])
+    known.start()
     for chunk in range(chunks):
-        for half in range(2):
-            piece(half, chunk).start()
-    first[...] = jnp.zeros_like(first)
+        piece(chunk).start()
+    ready = pltpu.make_async_copy(total_ref, first, in_sems.at[chunks])
+    ready.start()
+    written = [
+        pltpu.make_async_copy(first, out_ref.at[pl.ds(0, HALF)], out_sems.at[0]),
+        pltpu.make_async_copy(second, out_ref.at[pl.ds(HALF, HALF)], out_sems.at[1]),
+    ]
     second[...] = jnp.zeros_like(second)
+    known.wait()
     for chunk in range(chunks):
-        for half in range(2):
-            piece(half, chunk).wait()
+        piece(chunk).wait()
 
         @pl.loop(0, count, unroll=8)
         def _(index):
             slot = chunk * count + index
-            place = pl.ds(pl.multiple_of(wanted_ref[slot] * P_SIZE, P_SIZE), P_SIZE)
-            one = arrived[0, slot].astype(jnp.float32)
-            two = arrived[1, slot].astype(jnp.float32)
-            one_total, two_total = first[:, place], second[:, place]
-            first[:, place] = one_total + one
-            second[:, place] = two_total + two
-
-    written = []
-    for half, total in enumerate((first, second)):
-        rows = pl.ds(half * HALF, HALF)
-        written.append(pltpu.make_async_copy(total, out_ref.at[rows], out_sems.at[half]))
-        written[-1].start()
+            place = pl.ds(pl.multiple_of(wanted_ref[0, slot] * P_SIZE, P_SIZE), P_SIZE)
+            second[:, place] += arrived[slot].astype(jnp.float32)
+
+        if chunk == 1:
+            ready.wait()
+            written[0].start()
+
+    written[1].start()
     for copy in written:
         copy.wait()
 
@@ -417,15 +455,15 @@
     ends = 2 * slots
 
     anywhere = pl.BlockSpec(memory_space=pl.ANY)
-    smem = pl.BlockSpec(memory_space=pltpu.SMEM)
-    back, wanted = pl.pallas_call(
+    back, total, wanted = pl.pallas_call(
         functools.partial(exchange_kernel, groups, members, side),
         out_shape=[
-            jax.ShapeDtypeStruct((2, ends, HALF, P_SIZE), jnp.bfloat16),
-            jax.ShapeDtypeStruct((ends,), jnp.int32),
+            jax.ShapeDtypeStruct((ends, HALF, P_SIZE), jnp.bfloat16),
+            jax.ShapeDtypeStruct((HALF, local_count * P_SIZE), jnp.float32),
+            jax.ShapeDtypeStruct((1, ends), jnp.int32),
         ],
         in_specs=[anywhere, anywhere, anywhere, anywhere],
-        out_specs=[pl.BlockSpec(memory_space=pl.ANY), smem],
+        out_specs=[anywhere, anywhere, anywhere],
         scratch_shapes=[
             pltpu.VMEM((2, slots), jnp.int32),
             pltpu.VMEM((1, slots), jnp.int32),
@@ -445,33 +483,43 @@
             pltpu.VMEM((ends, HALF, P_SIZE), jnp.bfloat16),
             pltpu.VMEM((2, ends, HALF, P_SIZE), jnp.bfloat16),
             pltpu.VMEM((ends, P_SIZE, P_SIZE), jnp.bfloat16),
+            pltpu.SMEM((1, ends), jnp.int32),
+            pltpu.VMEM((1, ends), jnp.int32),
+            pltpu.VMEM((1, ends), jnp.int32),
+            pltpu.SMEM((1, ends), jnp.int32),
+            pltpu.VMEM((1, 128), jnp.int32),
+            pltpu.SMEM((1, 128), jnp.int32),
+            pltpu.VMEM((ends, HALF, P_SIZE), jnp.bfloat16),
+            pltpu.VMEM((ends, HALF, P_SIZE), jnp.float32),
+            pltpu.VMEM((HALF, local_count * P_SIZE), jnp.float32),
             pltpu.SemaphoreType.DMA((7,)),
             pltpu.SemaphoreType.DMA((7,)),
-            pltpu.SemaphoreType.DMA((8,)),
-            pltpu.SemaphoreType.DMA((8,)),
+            pltpu.SemaphoreType.DMA((members,)),
+            pltpu.SemaphoreType.DMA((members,)),
             pltpu.SemaphoreType.DMA,
             pltpu.SemaphoreType.DMA((4,)),
         ],
         compiler_params=pltpu.CompilerParams(
-            collective_id=0, has_side_effects=True, vmem_limit_bytes=56 * 1024 * 1024
+            collective_id=0, has_side_effects=True, vmem_limit_bytes=58 * 1024 * 1024
         ),
     )(pair_list.T, pair_kind.reshape(1, slots), modes, geometry)
 
-    chunks = min(8, ends // 8)
+    chunks = 4
     return pl.pallas_call(
         functools.partial(sum_kernel, chunks),
         out_shape=jax.ShapeDtypeStruct((2 * HALF, local_count * P_SIZE), jnp.float32),
-        in_specs=[smem, anywhere],
+        in_specs=[anywhere, anywhere, anywhere],
         out_specs=anywhere,
         scratch_shapes=[
-            pltpu.VMEM((2, ends, HALF, P_SIZE), jnp.bfloat16),
+            pltpu.SMEM((1, ends), jnp.int32),
+            pltpu.VMEM((ends, HALF, P_SIZE), jnp.bfloat16),
             pltpu.VMEM((HALF, local_count * P_SIZE), jnp.float32),
             pltpu.VMEM((HALF, local_count * P_SIZE), jnp.float32),
-            pltpu.SemaphoreType.DMA((2 * chunks,)),
+            pltpu.SemaphoreType.DMA((chunks + 2,)),
             pltpu.SemaphoreType.DMA((2,)),
         ],
-        compiler_params=pltpu.CompilerParams(vmem_limit_bytes=56 * 1024 * 1024),
-    )(wanted, back)
+        compiler_params=pltpu.CompilerParams(vmem_limit_bytes=58 * 1024 * 1024),
+    )(wanted, back, total)
 
 
 def solution(mesh):

time: 122 us -> 120 us (0.984)
  no operation moved by 1% of the time
where the time goes in v5:
time: 120 us
  Pallas kernels  120 us (100%)
    pallas_call x1, Pallas kernels, local(): pl.pallas_call(functools.partial(exchange_kernel, groups, members, side),...  116 us
    pallas_call x1, Pallas kernels, local(): pl.pallas_call(functools.partial(sum_kernel, chunks), out_shape=jax.Shape...  3.44 us

profile of v5, /device:TPU:1, one launch (start us, length us, event | category | flops | bytes accessed | tf_op | source)
XLA Modules:
  0.0 119.7 jit_solution(9924939488304391827)
XLA Ops:
  0.0 116.2 %shard_map.46 = (bf16[256,16,256]{2,1,0:T(8,128)(2,1)}, f32[16,16384]{1,0:T(8,128)}, s32[1,256]{1,0:T(1,128)}) custom-call(s32[2,128]{1,0:T(2,128)} %bitcast.2, s32[1,128]{1,0:T(1,128)} %bitcast.3, bf16[32,16384]{1,0:T(8,128)(2,1)} %modes_hbm.1, f32[4,16384]{1,0:T(4,128)} %geo_hbm.1), custom_call_target="tpu_custom_call" | custom-call | tf_op jit(solution)/shard_map/pallas_call | solution.py:458
  116.3 3.4 %shard_map.47 = f32[32,16384]{1,0:T(8,128)} custom-call(s32[1,256]{1,0:T(1,128)} %get-tuple-element.8.wanted_hbm, bf16[256,16,256]{2,1,0:T(8,128)(2,1)} %get-tuple-element.9.back_ref, f32[16,16384]{1,0:T(8,128)} %get-tuple-element.10.total_ref), custom_call_target="tpu_custom_call" | custom-call | tf_op jit(solution)/shard_map/pallas_call | solution.py:508

commit v6 on v5

--- a/solution.py
+++ b/solution.py
@@ -98,7 +98,7 @@
     side_bits = side.bit_length() - 1
 
     def partner_of(step):
-        shift = (step * 107) & (devices - 1)
+        shift = (step * 53) & (devices - 1)
         dg, dv = shift >> member_bits, shift & (members - 1)
         y = ((grp >> 1) + (dg >> 1)) & (groups // 2 - 1)
         core = (grp + dg) & 1

time: 120 us -> 119 us (level)
  no operation moved by 1% of the time
where the time goes in v6:
time: 119 us
  Pallas kernels  119 us (100%)
    pallas_call x1, Pallas kernels, local(): pl.pallas_call(functools.partial(exchange_kernel, groups, members, side),...  116 us
    pallas_call x1, Pallas kernels, local(): pl.pallas_call(functools.partial(sum_kernel, chunks), out_shape=jax.Shape...  3.44 us

profile of v6, /device:TPU:1, one launch (start us, length us, event | category | flops | bytes accessed | tf_op | source)
XLA Modules:
  0.0 119.2 jit_solution(1970492644889756845)
XLA Ops:
  0.0 115.7 %shard_map.46 = (bf16[256,16,256]{2,1,0:T(8,128)(2,1)}, f32[16,16384]{1,0:T(8,128)}, s32[1,256]{1,0:T(1,128)}) custom-call(s32[2,128]{1,0:T(2,128)} %bitcast.2, s32[1,128]{1,0:T(1,128)} %bitcast.3, bf16[32,16384]{1,0:T(8,128)(2,1)} %modes_hbm.1, f32[4,16384]{1,0:T(4,128)} %geo_hbm.1), custom_call_target="tpu_custom_call" | custom-call | tf_op jit(solution)/shard_map/pallas_call | solution.py:458
  115.8 3.4 %shard_map.47 = f32[32,16384]{1,0:T(8,128)} custom-call(s32[1,256]{1,0:T(1,128)} %get-tuple-element.8.wanted_hbm, bf16[256,16,256]{2,1,0:T(8,128)(2,1)} %get-tuple-element.9.back_ref, f32[16,16384]{1,0:T(8,128)} %get-tuple-element.10.total_ref), custom_call_target="tpu_custom_call" | custom-call | tf_op jit(solution)/shard_map/pallas_call | solution.py:508

commit v7 on v6

--- a/solution.py
+++ b/solution.py
@@ -165,6 +165,11 @@
     code_vmem[...] = table
     local = pltpu.make_async_copy(code_vmem, code_smem, local_sem)
     local.start()
+    pl.semaphore_wait(barrier, members + groups - 2)
+
+    for index in range(1, groups):
+        send(row_vmem, asked_vmem.at[my_key], 0, in_column(0, index))
+    in_own = drain(asked_vmem.at[pl.ds(0, groups - 1)], asked_vmem.at[pl.ds(0, groups - 1)], 0)
     high_rows = lax.broadcasted_iota(jnp.int32, (4, P_SIZE), 0)
     steps = jnp.where(high_rows < 3, X_STEPS, A_STEPS)
     inputs[2].wait()
@@ -175,11 +180,6 @@
         mode_blocks[1, cluster] = modes_ref[HALF : 2 * HALF, panels]
         geo_blocks[cluster] = jnp.round(geo_ref[:, panels] * steps)
     local.wait()
-    pl.semaphore_wait(barrier, members + groups - 2)
-
-    for index in range(1, groups):
-        send(row_vmem, asked_vmem.at[my_key], 0, in_column(0, index))
-    in_own = drain(asked_vmem.at[pl.ds(0, groups - 1)], asked_vmem.at[pl.ds(0, groups - 1)], 0)
     in_own.wait_recv()
 
     def across(which, mark):

time: 119 us -> 119 us (level)
  no operation moved by 1% of the time
where the time goes in v7:
time: 119 us
  Pallas kernels  119 us (100%)
    pallas_call x1, Pallas kernels, local(): pl.pallas_call(functools.partial(exchange_kernel, groups, members, side),...  116 us
    pallas_call x1, Pallas kernels, local(): pl.pallas_call(functools.partial(sum_kernel, chunks), out_shape=jax.Shape...  3.44 us

profile of v7, /device:TPU:1, one launch (start us, length us, event | category | flops | bytes accessed | tf_op | source)
XLA Modules:
  0.0 119.2 jit_solution(12447161276140152712)
XLA Ops:
  0.0 115.8 %shard_map.46 = (bf16[256,16,256]{2,1,0:T(8,128)(2,1)}, f32[16,16384]{1,0:T(8,128)}, s32[1,256]{1,0:T(1,128)}) custom-call(s32[2,128]{1,0:T(2,128)} %bitcast.2, s32[1,128]{1,0:T(1,128)} %bitcast.3, bf16[32,16384]{1,0:T(8,128)(2,1)} %modes_hbm.1, f32[4,16384]{1,0:T(4,128)} %geo_hbm.1), custom_call_target="tpu_custom_call" | custom-call | tf_op jit(solution)/shard_map/pallas_call | solution.py:458
  115.8 3.4 %shard_map.47 = f32[32,16384]{1,0:T(8,128)} custom-call(s32[1,256]{1,0:T(1,128)} %get-tuple-element.8.wanted_hbm, bf16[256,16,256]{2,1,0:T(8,128)(2,1)} %get-tuple-element.9.back_ref, f32[16,16384]{1,0:T(8,128)} %get-tuple-element.10.total_ref), custom_call_target="tpu_custom_call" | custom-call | tf_op jit(solution)/shard_map/pallas_call | solution.py:508
